TPU v7x, 256 devices: a whole 4x4x8 slice. The times are simulated.
256 devices in a mesh: ctx: 128 (over x, y, z), kvh: 2 (over core).
Axes of the slice: x: 4, y: 4, z: 8, core: 2. Of those that a mesh axis runs over, the one named last changes fastest.
Arguments:
- queries: bfloat16 [32768, 4096], P('ctx', 'kvh'), may hold values from -5 to 5
- keys: bfloat16 [32768, 1024], P('ctx', 'kvh'), may hold values from -5 to 5
- values: bfloat16 [32768, 1024], P('ctx', 'kvh'), may hold values from -5 to 5
- segment_ids: int32 [32768], P('ctx'), may hold values from 0 to 255, never falling along the last dimension, each value on 1 to 4096 neighbouring positions
Outputs:
- attended: bfloat16 [32768, 4096], P(('ctx', 'kvh'))
Inputs may be any that keep to these rules, and one draw needn't show every extreme that they name: `segment_ids`: every document has at most 4096 tokens.
All inputs are finite; a program needn't handle non-finite values.
Results may differ from a plain program's by a relative error of at most 0.005.
Values may be sent and summed in bfloat16 or wider, within the bound.
A program may use at most 128 MiB of HBM per device.

v0:
```python
import jax
import jax.numpy as jnp
from jax import lax
from jax.sharding import PartitionSpec as P

HEAD_DIMENSION = 128


def passed_along(value, axis, by):
    size = lax.axis_size(axis)
    pairs = [(i, i + by) for i in range(size) if 0 <= i + by < size]
    return lax.ppermute(value, axis, pairs)


def per_device(queries, keys, values, segment_ids):
    tok_rows = queries.shape[0]
    ctx_count = lax.axis_size("ctx")
    reach_blocks = min(16, ctx_count // 4)
    near_half = reach_blocks // 2
    far_count = reach_blocks - near_half
    my_index = lax.axis_index("ctx")
    kv_heads = keys.shape[1] // HEAD_DIMENSION
    query_group = queries.shape[1] // keys.shape[1]
    scale_factor = HEAD_DIMENSION ** (-0.5)
    own_heads = queries.reshape(tok_rows, kv_heads, query_group, HEAD_DIMENSION)
    positions = jnp.arange(tok_rows, dtype=jnp.int32)
    seg_window = segment_ids[None]
    held_ids = 1
    while held_ids < reach_blocks + 1:
        send_ids = min(held_ids, reach_blocks + 1 - held_ids)
        arrived_ids = passed_along(seg_window[:send_ids], "ctx", held_ids)
        seg_window = jnp.concatenate([seg_window, arrived_ids], axis=0)
        held_ids = held_ids + send_ids

    def compute_tile(carry_state, q_heads, query_seg, kv_block, distance, key_seg):
        row_peak, denom_sum, accum_out = carry_state
        k_heads = kv_block[0].reshape(tok_rows, kv_heads, HEAD_DIMENSION)
        v_heads = kv_block[1].reshape(tok_rows, kv_heads, HEAD_DIMENSION)
        scores = (
            jnp.einsum("tgqd,sgd->tgqs", q_heads, k_heads, preferred_element_type=jnp.float32)
            * scale_factor
        )
        allowed = (query_seg[:, None] == key_seg[None, :]) & (
            positions[:, None] + distance * tok_rows >= positions[None, :]
        )
        scores = jnp.where(allowed[:, None, None, :], scores, -jnp.inf)
        new_peak = jnp.maximum(row_peak, jnp.max(scores, axis=-1))
        fading = jnp.exp(row_peak - new_peak)
        weights_p = jnp.exp(scores - new_peak[..., None])
        denom_sum = denom_sum * fading + jnp.sum(weights_p, axis=-1)
        accum_out = accum_out * fading[..., None] + jnp.einsum(
            "tgqs,sgd->tgqd",
            weights_p.astype(jnp.bfloat16),
            v_heads,
            preferred_element_type=jnp.float32,
        )
        return (new_peak, denom_sum, accum_out)

    def attend(carry_state, q_heads, window_ids, owner, kv_block, distance, dropped):
        query_seg = window_ids[0]
        source = owner - distance
        key_seg = lax.dynamic_index_in_dim(window_ids, distance, 0, keepdims=False)
        live = (source >= 0) & jnp.logical_not(dropped)
        key_seg = jnp.where(live, key_seg, -1)
        return compute_tile(carry_state, q_heads, query_seg, kv_block, distance, key_seg)

    give_away = jnp.array(False)

    def own_attend(carry_state, kv_block, distance):
        dropped = give_away & (distance > near_half)
        return attend(carry_state, own_heads, seg_window, my_index, kv_block, distance, dropped)

    kv_pair = jnp.stack((keys, values))
    carry_state = compute_tile(
        (
            jnp.full((tok_rows, kv_heads, query_group), -1e30, jnp.float32),
            jnp.zeros((tok_rows, kv_heads, query_group), jnp.float32),
            jnp.zeros((tok_rows, kv_heads, query_group, HEAD_DIMENSION), jnp.float32),
        ),
        own_heads,
        segment_ids,
        kv_pair,
        0,
        segment_ids,
    )
    far_buffer = jnp.zeros((far_count,) + kv_pair.shape, kv_pair.dtype)

    def chain_turn(turn_index, carry):
        held_state, moving, stored = carry
        moving = passed_along(moving, "ctx", 1)
        slot = jnp.clip(turn_index - near_half - 1, 0, far_count - 1)
        updated = lax.dynamic_update_index_in_dim(stored, moving, slot, 0)
        stored = jnp.where(turn_index > near_half, updated, stored)
        return (own_attend(held_state, moving, turn_index), moving, stored)

    carry_state, kv_last, far_buffer = lax.fori_loop(
        1, reach_blocks + 1, chain_turn, (carry_state, kv_pair, far_buffer)
    )
    row_peak, denom_sum, accum_out = carry_state
    mixed = (
        (accum_out / denom_sum[..., None])
        .astype(jnp.bfloat16)
        .reshape(tok_rows, kv_heads * query_group * HEAD_DIMENSION)
    )
    return lax.all_to_all(mixed, "kvh", split_axis=0, concat_axis=1, tiled=True)


def solution(mesh):
    return jax.shard_map(
        per_device,
        mesh=mesh,
        in_specs=(P("ctx", "kvh"), P("ctx", "kvh"), P("ctx", "kvh"), P("ctx")),
        out_specs=P(("ctx", "kvh"), None),
        check_vma=False,
    )
```

profile of v0, /device:TPU:6, one launch (start us, length us, event | category | flops | bytes accessed | tf_op | source)
XLA Modules:
  0.0 414.2 jit_solution(18122673408477337433)
XLA Ops:
  0.0 5.1 %collective-permute-start.5 = (s32[1,256]{1,0:T(1,128)}, s32[1,256]{1,0:T(1,128)S(1)}, u32[]{:S(2)}, u32[]{:S(2)}) collective-permute-start(s32[1,256]{1,0:T(1,128)} %bitcast.103), channel_id=1, source_target_pairs={{0,32},{2,34},{4,36},{6,38},{8,40},{10,42},{12,44},{14,46},{16,48}... | collective-permute-start | bytes 3080 | tf_op jit(solution)/shard_map/ppermute | solution.py:12
  5.1 3.8 collective-permute-start.1
  16.0 5.2 %collective-permute-start.2 = (s32[2,256]{1,0:T(2,128)S(1)}, s32[2,256]{1,0:T(2,128)S(1)}, u32[]{:S(2)}, u32[]{:S(2)}) collective-permute-start(s32[2,256]{1,0:T(2,128)S(1)} %pad_add_fusion.2), channel_id=1, source_target_pairs={{0,4},{2,6},{4,8},{6,10},{8,12},{10,14},{12,16},{14,18},{16,20},{1... | collective-permute-start | bytes 6152 | tf_op jit(solution)/shard_map/ppermute | solution.py:12
  22.1 4.6 %collective-permute-done.2 = s32[2,256]{1,0:T(2,128)S(1)} collective-permute-done((s32[2,256]{1,0:T(2,128)S(1)}, s32[2,256]{1,0:T(2,128)S(1)}, u32[]{:S(2)}, u32[]{:S(2)}) %collective-permute-start.2) | collective-permute-done | bytes 2080 | tf_op jit(solution)/shard_map/ppermute | solution.py:12
  26.6 5.2 %collective-permute-start.3 = (s32[4,256]{1,0:T(4,128)S(1)}, s32[4,256]{1,0:T(4,128)S(1)}, u32[]{:S(2)}, u32[]{:S(2)}) collective-permute-start(s32[4,256]{1,0:T(4,128)S(1)} %pad_add_fusion.1), channel_id=1, source_target_pairs={{0,8},{2,10},{4,12},{6,14},{8,16},{10,18},{12,20},{14,22},{16,24},... | collective-permute-start | bytes 12296 | tf_op jit(solution)/shard_map/ppermute | solution.py:12
  31.9 3.3 bitcast_add_fusion.1
  44.1 2.6 collective-permute-done.4
  46.7 358.5 %while.23 = (s32[]{:T(128)}, f32[256,4,4]{0,2,1:T(4,128)S(1)}, f32[256,4,4]{0,2,1:T(4,128)S(1)}, f32[256,4,4,128]{3,0,2,1:T(8,128)S(1)}, bf16[2,256,512]{1,2,0:T...) while((s32[]{:T(128)}, f32[256,4,4]{0,2,1:T(4,128)S(1)}, ...), condition=%wide.region_5.6_spmd.clone.clone, body=%wide.region_2.5_spmd.clone.clone.sunk | while | flops 549659136 | bytes 23075056 | solution.py:96
  46.7 3.9 collective-permute-start
  50.8 12.0 %collective-permute-done = bf16[2,256,512]{1,2,0:T(8,128)(2,1)S(1)} collective-permute-done((bf16[2,256,512]{1,2,0:T(8,128)(2,1)}, bf16[2,256,512]{1,2,0:T(8,128)(2,1)S(1)}, u32[]{:S(2)}, u32[]{:S(2)}) %collective-permute-start) | collective-permute-done | bytes 524320 | tf_op jit(solution)/shard_map/while/body/eval_jaxpr/ppermute | solution.py:12
  70.5 13.4 %collective-permute-done = bf16[2,256,512]{1,2,0:T(8,128)(2,1)S(1)} collective-permute-done((bf16[2,256,512]{1,2,0:T(8,128)(2,1)}, bf16[2,256,512]{1,2,0:T(8,128)(2,1)S(1)}, u32[]{:S(2)}, u32[]{:S(2)}) %collective-permute-start) | collective-permute-done | bytes 524320 | tf_op jit(solution)/shard_map/while/body/eval_jaxpr/ppermute | solution.py:12
  84.0 2.1 fusion.53
  91.6 13.4 %collective-permute-done = bf16[2,256,512]{1,2,0:T(8,128)(2,1)S(1)} collective-permute-done((bf16[2,256,512]{1,2,0:T(8,128)(2,1)}, bf16[2,256,512]{1,2,0:T(8,128)(2,1)S(1)}, u32[]{:S(2)}, u32[]{:S(2)}) %collective-permute-start) | collective-permute-done | bytes 524320 | tf_op jit(solution)/shard_map/while/body/eval_jaxpr/ppermute | solution.py:12
  112.8 13.4 %collective-permute-done = bf16[2,256,512]{1,2,0:T(8,128)(2,1)S(1)} collective-permute-done((bf16[2,256,512]{1,2,0:T(8,128)(2,1)}, bf16[2,256,512]{1,2,0:T(8,128)(2,1)S(1)}, u32[]{:S(2)}, u32[]{:S(2)}) %collective-permute-start) | collective-permute-done | bytes 524320 | tf_op jit(solution)/shard_map/while/body/eval_jaxpr/ppermute | solution.py:12
  126.2 2.1 fusion.53
  133.9 13.4 %collective-permute-done = bf16[2,256,512]{1,2,0:T(8,128)(2,1)S(1)} collective-permute-done((bf16[2,256,512]{1,2,0:T(8,128)(2,1)}, bf16[2,256,512]{1,2,0:T(8,128)(2,1)S(1)}, u32[]{:S(2)}, u32[]{:S(2)}) %collective-permute-start) | collective-permute-done | bytes 524320 | tf_op jit(solution)/shard_map/while/body/eval_jaxpr/ppermute | solution.py:12
  155.0 13.4 %collective-permute-done = bf16[2,256,512]{1,2,0:T(8,128)(2,1)S(1)} collective-permute-done((bf16[2,256,512]{1,2,0:T(8,128)(2,1)}, bf16[2,256,512]{1,2,0:T(8,128)(2,1)S(1)}, u32[]{:S(2)}, u32[]{:S(2)}) %collective-permute-start) | collective-permute-done | bytes 524320 | tf_op jit(solution)/shard_map/while/body/eval_jaxpr/ppermute | solution.py:12
  176.2 13.4 %collective-permute-done = bf16[2,256,512]{1,2,0:T(8,128)(2,1)S(1)} collective-permute-done((bf16[2,256,512]{1,2,0:T(8,128)(2,1)}, bf16[2,256,512]{1,2,0:T(8,128)(2,1)S(1)}, u32[]{:S(2)}, u32[]{:S(2)}) %collective-permute-start) | collective-permute-done | bytes 524320 | tf_op jit(solution)/shard_map/while/body/eval_jaxpr/ppermute | solution.py:12
  189.6 2.1 fusion.53
  197.3 13.4 %collective-permute-done = bf16[2,256,512]{1,2,0:T(8,128)(2,1)S(1)} collective-permute-done((bf16[2,256,512]{1,2,0:T(8,128)(2,1)}, bf16[2,256,512]{1,2,0:T(8,128)(2,1)S(1)}, u32[]{:S(2)}, u32[]{:S(2)}) %collective-permute-start) | collective-permute-done | bytes 524320 | tf_op jit(solution)/shard_map/while/body/eval_jaxpr/ppermute | solution.py:12
  218.5 13.4 %collective-permute-done = bf16[2,256,512]{1,2,0:T(8,128)(2,1)S(1)} collective-permute-done((bf16[2,256,512]{1,2,0:T(8,128)(2,1)}, bf16[2,256,512]{1,2,0:T(8,128)(2,1)S(1)}, u32[]{:S(2)}, u32[]{:S(2)}) %collective-permute-start) | collective-permute-done | bytes 524320 | tf_op jit(solution)/shard_map/while/body/eval_jaxpr/ppermute | solution.py:12
  231.9 2.1 fusion.53
  239.6 14.2 %collective-permute-done = bf16[2,256,512]{1,2,0:T(8,128)(2,1)S(1)} collective-permute-done((bf16[2,256,512]{1,2,0:T(8,128)(2,1)}, bf16[2,256,512]{1,2,0:T(8,128)(2,1)S(1)}, u32[]{:S(2)}, u32[]{:S(2)}) %collective-permute-start) | collective-permute-done | bytes 524320 | tf_op jit(solution)/shard_map/while/body/eval_jaxpr/ppermute | solution.py:12
  261.5 15.3 %collective-permute-done = bf16[2,256,512]{1,2,0:T(8,128)(2,1)S(1)} collective-permute-done((bf16[2,256,512]{1,2,0:T(8,128)(2,1)}, bf16[2,256,512]{1,2,0:T(8,128)(2,1)S(1)}, u32[]{:S(2)}, u32[]{:S(2)}) %collective-permute-start) | collective-permute-done | bytes 524320 | tf_op jit(solution)/shard_map/while/body/eval_jaxpr/ppermute | solution.py:12
  284.5 16.4 %collective-permute-done = bf16[2,256,512]{1,2,0:T(8,128)(2,1)S(1)} collective-permute-done((bf16[2,256,512]{1,2,0:T(8,128)(2,1)}, bf16[2,256,512]{1,2,0:T(8,128)(2,1)S(1)}, u32[]{:S(2)}, u32[]{:S(2)}) %collective-permute-start) | collective-permute-done | bytes 524320 | tf_op jit(solution)/shard_map/while/body/eval_jaxpr/ppermute | solution.py:12
  308.6 17.5 %collective-permute-done = bf16[2,256,512]{1,2,0:T(8,128)(2,1)S(1)} collective-permute-done((bf16[2,256,512]{1,2,0:T(8,128)(2,1)}, bf16[2,256,512]{1,2,0:T(8,128)(2,1)S(1)}, u32[]{:S(2)}, u32[]{:S(2)}) %collective-permute-start) | collective-permute-done | bytes 524320 | tf_op jit(solution)/shard_map/while/body/eval_jaxpr/ppermute | solution.py:12
  326.1 2.1 fusion.53
  333.8 18.7 %collective-permute-done = bf16[2,256,512]{1,2,0:T(8,128)(2,1)S(1)} collective-permute-done((bf16[2,256,512]{1,2,0:T(8,128)(2,1)}, bf16[2,256,512]{1,2,0:T(8,128)(2,1)S(1)}, u32[]{:S(2)}, u32[]{:S(2)}) %collective-permute-start) | collective-permute-done | bytes 524320 | tf_op jit(solution)/shard_map/while/body/eval_jaxpr/ppermute | solution.py:12
  360.2 18.2 %collective-permute-done = bf16[2,256,512]{1,2,0:T(8,128)(2,1)S(1)} collective-permute-done((bf16[2,256,512]{1,2,0:T(8,128)(2,1)}, bf16[2,256,512]{1,2,0:T(8,128)(2,1)S(1)}, u32[]{:S(2)}, u32[]{:S(2)}) %collective-permute-start) | collective-permute-done | bytes 524320 | tf_op jit(solution)/shard_map/while/body/eval_jaxpr/ppermute | solution.py:12
  378.5 2.1 fusion.53
  386.2 13.4 %collective-permute-done = bf16[2,256,512]{1,2,0:T(8,128)(2,1)S(1)} collective-permute-done((bf16[2,256,512]{1,2,0:T(8,128)(2,1)}, bf16[2,256,512]{1,2,0:T(8,128)(2,1)S(1)}, u32[]{:S(2)}, u32[]{:S(2)}) %collective-permute-start) | collective-permute-done | bytes 524320 | tf_op jit(solution)/shard_map/while/body/eval_jaxpr/ppermute | solution.py:12
  407.6 4.6 %all_to_all.19 = bf16[2,128,2048]{2,1,0:T(8,128)(2,1)S(1)} all-to-all(bf16[2,128,2048]{2,1,0:T(8,128)(2,1)S(1)} %all_to_all.14), channel_id=1, replica_groups=mesh['ctx'=128,'kvh'=2] {'kvh'}, dimensions={0} | all-to-all | bytes 2097152 | tf_op jit(solution)/shard_map/all_to_all | solution.py:105
  (218 shorter events, 128.8 us)
Async XLA Ops:
  0.0 44.1 %collective-permute-start.5 = (s32[1,256]{1,0:T(1,128)}, s32[1,256]{1,0:T(1,128)S(1)}, u32[]{:S(2)}, u32[]{:S(2)}) collective-permute-start(s32[1,256]{1,0:T(1,128)} %bitcast.103), channel_id=1, source_target_pairs={{0,32},{2,34},{4,36},{6,38},{8,40},{10,42},{12,44},{14,46},{16,48}... | collective-permute-start | bytes 3080 | tf_op jit(solution)/shard_map/ppermute | solution.py:12
  5.1 10.9 %collective-permute-start.1 = (s32[1,256]{1,0:T(1,128)}, s32[1,256]{1,0:T(1,128)S(1)}, u32[]{:S(2)}, u32[]{:S(2)}) collective-permute-start(s32[1,256]{1,0:T(1,128)} %bitcast.104), channel_id=1, source_target_pairs={{0,2},{2,4},{4,6},{6,8},{8,10},{10,12},{12,14},{14,16},{16,18},{18... | collective-permute-start | bytes 3080 | tf_op jit(solution)/shard_map/ppermute | solution.py:12
  12.3 3.7 copy-start.3
  12.3 9.0 %copy-start.2 = (bf16[256,512]{1,0:T(8,128)(2,1)S(1)}, bf16[256,512]{1,0:T(8,128)(2,1)}, u32[]{:S(2)}) copy-start(bf16[256,512]{1,0:T(8,128)(2,1)} %param.8) | copy-start | bytes 786436
  13.1 1.9 copy-start
  15.9 19.3 %copy-start.1 = (bf16[256,512]{1,0:T(8,128)(2,1)S(1)}, bf16[256,512]{1,0:T(8,128)(2,1)}, u32[]{:S(2)}) copy-start(bf16[256,512]{1,0:T(8,128)(2,1)} %param.7) | copy-start | bytes 786436
  16.0 10.6 %collective-permute-start.2 = (s32[2,256]{1,0:T(2,128)S(1)}, s32[2,256]{1,0:T(2,128)S(1)}, u32[]{:S(2)}, u32[]{:S(2)}) collective-permute-start(s32[2,256]{1,0:T(2,128)S(1)} %pad_add_fusion.2), channel_id=1, source_target_pairs={{0,4},{2,6},{4,8},{6,10},{8,12},{10,14},{12,16},{14,18},{16,20},{1... | collective-permute-start | bytes 6152 | tf_op jit(solution)/shard_map/ppermute | solution.py:12
  26.6 12.4 %collective-permute-start.3 = (s32[4,256]{1,0:T(4,128)S(1)}, s32[4,256]{1,0:T(4,128)S(1)}, u32[]{:S(2)}, u32[]{:S(2)}) collective-permute-start(s32[4,256]{1,0:T(4,128)S(1)} %pad_add_fusion.1), channel_id=1, source_target_pairs={{0,8},{2,10},{4,12},{6,14},{8,16},{10,18},{12,20},{14,22},{16,24},... | collective-permute-start | bytes 12296 | tf_op jit(solution)/shard_map/ppermute | solution.py:12
  39.1 7.7 %collective-permute-start.4 = (s32[8,256]{1,0:T(8,128)S(1)}, s32[8,256]{1,0:T(8,128)S(1)}, u32[]{:S(2)}, u32[]{:S(2)}) collective-permute-start(s32[8,256]{1,0:T(8,128)S(1)} %pad_add_fusion), channel_id=1, source_target_pairs={{0,16},{2,18},{4,20},{6,22},{8,24},{10,26},{12,28},{14,30},{16,32}... | collective-permute-start | bytes 24584 | tf_op jit(solution)/shard_map/ppermute | solution.py:12
  46.7 16.0 %collective-permute-start = (bf16[2,256,512]{1,2,0:T(8,128)(2,1)}, bf16[2,256,512]{1,2,0:T(8,128)(2,1)S(1)}, u32[]{:S(2)}, u32[]{:S(2)}) collective-permute-start(bf16[2,256,512]{1,2,0:T(8,128)(2,1)} %get-tuple-element.431), channel_id=1, source_target_pairs={{0,2},{2,4},{4,6},{6,8},{8,10},{10,12},{12,14},{14,16},{16,18},{18... | collective-permute-start | bytes 1572872 | tf_op jit(solution)/shard_map/while/body/eval_jaxpr/ppermute | solution.py:12
  68.4 15.5 %collective-permute-start = (bf16[2,256,512]{1,2,0:T(8,128)(2,1)}, bf16[2,256,512]{1,2,0:T(8,128)(2,1)S(1)}, u32[]{:S(2)}, u32[]{:S(2)}) collective-permute-start(bf16[2,256,512]{1,2,0:T(8,128)(2,1)} %get-tuple-element.431), channel_id=1, source_target_pairs={{0,2},{2,4},{4,6},{6,8},{8,10},{10,12},{12,14},{14,16},{16,18},{18... | collective-permute-start | bytes 1572872 | tf_op jit(solution)/shard_map/while/body/eval_jaxpr/ppermute | solution.py:12
  89.6 15.5 %collective-permute-start = (bf16[2,256,512]{1,2,0:T(8,128)(2,1)}, bf16[2,256,512]{1,2,0:T(8,128)(2,1)S(1)}, u32[]{:S(2)}, u32[]{:S(2)}) collective-permute-start(bf16[2,256,512]{1,2,0:T(8,128)(2,1)} %get-tuple-element.431), channel_id=1, source_target_pairs={{0,2},{2,4},{4,6},{6,8},{8,10},{10,12},{12,14},{14,16},{16,18},{18... | collective-permute-start | bytes 1572872 | tf_op jit(solution)/shard_map/while/body/eval_jaxpr/ppermute | solution.py:12
  110.7 15.5 %collective-permute-start = (bf16[2,256,512]{1,2,0:T(8,128)(2,1)}, bf16[2,256,512]{1,2,0:T(8,128)(2,1)S(1)}, u32[]{:S(2)}, u32[]{:S(2)}) collective-permute-start(bf16[2,256,512]{1,2,0:T(8,128)(2,1)} %get-tuple-element.431), channel_id=1, source_target_pairs={{0,2},{2,4},{4,6},{6,8},{8,10},{10,12},{12,14},{14,16},{16,18},{18... | collective-permute-start | bytes 1572872 | tf_op jit(solution)/shard_map/while/body/eval_jaxpr/ppermute | solution.py:12
  131.8 15.5 %collective-permute-start = (bf16[2,256,512]{1,2,0:T(8,128)(2,1)}, bf16[2,256,512]{1,2,0:T(8,128)(2,1)S(1)}, u32[]{:S(2)}, u32[]{:S(2)}) collective-permute-start(bf16[2,256,512]{1,2,0:T(8,128)(2,1)} %get-tuple-element.431), channel_id=1, source_target_pairs={{0,2},{2,4},{4,6},{6,8},{8,10},{10,12},{12,14},{14,16},{16,18},{18... | collective-permute-start | bytes 1572872 | tf_op jit(solution)/shard_map/while/body/eval_jaxpr/ppermute | solution.py:12
  153.0 15.5 %collective-permute-start = (bf16[2,256,512]{1,2,0:T(8,128)(2,1)}, bf16[2,256,512]{1,2,0:T(8,128)(2,1)S(1)}, u32[]{:S(2)}, u32[]{:S(2)}) collective-permute-start(bf16[2,256,512]{1,2,0:T(8,128)(2,1)} %get-tuple-element.431), channel_id=1, source_target_pairs={{0,2},{2,4},{4,6},{6,8},{8,10},{10,12},{12,14},{14,16},{16,18},{18... | collective-permute-start | bytes 1572872 | tf_op jit(solution)/shard_map/while/body/eval_jaxpr/ppermute | solution.py:12
  174.1 15.5 %collective-permute-start = (bf16[2,256,512]{1,2,0:T(8,128)(2,1)}, bf16[2,256,512]{1,2,0:T(8,128)(2,1)S(1)}, u32[]{:S(2)}, u32[]{:S(2)}) collective-permute-start(bf16[2,256,512]{1,2,0:T(8,128)(2,1)} %get-tuple-element.431), channel_id=1, source_target_pairs={{0,2},{2,4},{4,6},{6,8},{8,10},{10,12},{12,14},{14,16},{16,18},{18... | collective-permute-start | bytes 1572872 | tf_op jit(solution)/shard_map/while/body/eval_jaxpr/ppermute | solution.py:12
  195.2 15.5 %collective-permute-start = (bf16[2,256,512]{1,2,0:T(8,128)(2,1)}, bf16[2,256,512]{1,2,0:T(8,128)(2,1)S(1)}, u32[]{:S(2)}, u32[]{:S(2)}) collective-permute-start(bf16[2,256,512]{1,2,0:T(8,128)(2,1)} %get-tuple-element.431), channel_id=1, source_target_pairs={{0,2},{2,4},{4,6},{6,8},{8,10},{10,12},{12,14},{14,16},{16,18},{18... | collective-permute-start | bytes 1572872 | tf_op jit(solution)/shard_map/while/body/eval_jaxpr/ppermute | solution.py:12
  216.4 15.5 %collective-permute-start = (bf16[2,256,512]{1,2,0:T(8,128)(2,1)}, bf16[2,256,512]{1,2,0:T(8,128)(2,1)S(1)}, u32[]{:S(2)}, u32[]{:S(2)}) collective-permute-start(bf16[2,256,512]{1,2,0:T(8,128)(2,1)} %get-tuple-element.431), channel_id=1, source_target_pairs={{0,2},{2,4},{4,6},{6,8},{8,10},{10,12},{12,14},{14,16},{16,18},{18... | collective-permute-start | bytes 1572872 | tf_op jit(solution)/shard_map/while/body/eval_jaxpr/ppermute | solution.py:12
  237.5 16.3 %collective-permute-start = (bf16[2,256,512]{1,2,0:T(8,128)(2,1)}, bf16[2,256,512]{1,2,0:T(8,128)(2,1)S(1)}, u32[]{:S(2)}, u32[]{:S(2)}) collective-permute-start(bf16[2,256,512]{1,2,0:T(8,128)(2,1)} %get-tuple-element.431), channel_id=1, source_target_pairs={{0,2},{2,4},{4,6},{6,8},{8,10},{10,12},{12,14},{14,16},{16,18},{18... | collective-permute-start | bytes 1572872 | tf_op jit(solution)/shard_map/while/body/eval_jaxpr/ppermute | solution.py:12
  259.5 17.4 %collective-permute-start = (bf16[2,256,512]{1,2,0:T(8,128)(2,1)}, bf16[2,256,512]{1,2,0:T(8,128)(2,1)S(1)}, u32[]{:S(2)}, u32[]{:S(2)}) collective-permute-start(bf16[2,256,512]{1,2,0:T(8,128)(2,1)} %get-tuple-element.431), channel_id=1, source_target_pairs={{0,2},{2,4},{4,6},{6,8},{8,10},{10,12},{12,14},{14,16},{16,18},{18... | collective-permute-start | bytes 1572872 | tf_op jit(solution)/shard_map/while/body/eval_jaxpr/ppermute | solution.py:12
  282.5 18.4 %collective-permute-start = (bf16[2,256,512]{1,2,0:T(8,128)(2,1)}, bf16[2,256,512]{1,2,0:T(8,128)(2,1)S(1)}, u32[]{:S(2)}, u32[]{:S(2)}) collective-permute-start(bf16[2,256,512]{1,2,0:T(8,128)(2,1)} %get-tuple-element.431), channel_id=1, source_target_pairs={{0,2},{2,4},{4,6},{6,8},{8,10},{10,12},{12,14},{14,16},{16,18},{18... | collective-permute-start | bytes 1572872 | tf_op jit(solution)/shard_map/while/body/eval_jaxpr/ppermute | solution.py:12
  306.6 19.5 %collective-permute-start = (bf16[2,256,512]{1,2,0:T(8,128)(2,1)}, bf16[2,256,512]{1,2,0:T(8,128)(2,1)S(1)}, u32[]{:S(2)}, u32[]{:S(2)}) collective-permute-start(bf16[2,256,512]{1,2,0:T(8,128)(2,1)} %get-tuple-element.431), channel_id=1, source_target_pairs={{0,2},{2,4},{4,6},{6,8},{8,10},{10,12},{12,14},{14,16},{16,18},{18... | collective-permute-start | bytes 1572872 | tf_op jit(solution)/shard_map/while/body/eval_jaxpr/ppermute | solution.py:12
  331.7 20.8 %collective-permute-start = (bf16[2,256,512]{1,2,0:T(8,128)(2,1)}, bf16[2,256,512]{1,2,0:T(8,128)(2,1)S(1)}, u32[]{:S(2)}, u32[]{:S(2)}) collective-permute-start(bf16[2,256,512]{1,2,0:T(8,128)(2,1)} %get-tuple-element.431), channel_id=1, source_target_pairs={{0,2},{2,4},{4,6},{6,8},{8,10},{10,12},{12,14},{14,16},{16,18},{18... | collective-permute-start | bytes 1572872 | tf_op jit(solution)/shard_map/while/body/eval_jaxpr/ppermute | solution.py:12
  358.1 20.3 %collective-permute-start = (bf16[2,256,512]{1,2,0:T(8,128)(2,1)}, bf16[2,256,512]{1,2,0:T(8,128)(2,1)S(1)}, u32[]{:S(2)}, u32[]{:S(2)}) collective-permute-start(bf16[2,256,512]{1,2,0:T(8,128)(2,1)} %get-tuple-element.431), channel_id=1, source_target_pairs={{0,2},{2,4},{4,6},{6,8},{8,10},{10,12},{12,14},{14,16},{16,18},{18... | collective-permute-start | bytes 1572872 | tf_op jit(solution)/shard_map/while/body/eval_jaxpr/ppermute | solution.py:12
  384.1 15.5 %collective-permute-start = (bf16[2,256,512]{1,2,0:T(8,128)(2,1)}, bf16[2,256,512]{1,2,0:T(8,128)(2,1)S(1)}, u32[]{:S(2)}, u32[]{:S(2)}) collective-permute-start(bf16[2,256,512]{1,2,0:T(8,128)(2,1)} %get-tuple-element.431), channel_id=1, source_target_pairs={{0,2},{2,4},{4,6},{6,8},{8,10},{10,12},{12,14},{14,16},{16,18},{18... | collective-permute-start | bytes 1572872 | tf_op jit(solution)/shard_map/while/body/eval_jaxpr/ppermute | solution.py:12
where the time goes:
time: 416 us; the launch traced here: 414 us
  waiting for transfers between devices  242 us (58%)
  matrix products  66 us (16%)
  starting transfers between devices  53.8 us (13%)
  local copies, waits for them, and re-layouts  25.4 us (6%)
  other arithmetic  20.6 us (5%)
  blocking collectives  4.58 us (1%)
    ppermute x21, waiting for transfers between devices, passed_along(): return lax.ppermute(value, axis, pairs)  242 us
    ppermute x21, starting transfers between devices, passed_along(): return lax.ppermute(value, axis, pairs)  53.8 us
    dot_general x17, matrix products, compute_tile(): jnp.einsum('tgqd,sgd->tgqs', q_heads, k_heads, preferred_element_type=jnp...  34.1 us
    dot_general x17, matrix products, compute_tile(): jnp.einsum('tgqs,sgd->tgqd', weights_p.astype(jnp.bfloat16), v_heads, pre...  31.8 us
    reduce_sum x17, other arithmetic, compute_tile(): denom_sum = denom_sum * fading + jnp.sum(weights_p, axis=-1)  15 us
    while x32, local copies, waits for them, and re-layouts  12.8 us
  transfers between devices with their start and end apart: 21, of which 20 were waited for; matrix products, arithmetic and copies ran while one was open for 4% of the time, Pallas kernels for 0%

commit v1 on v0

v1 whole, which is shorter than its diff:
```python
import jax
import jax.numpy as jnp
from jax import lax
from jax.experimental import pallas as pl
from jax.experimental.pallas import tpu as pltpu
from jax.sharding import PartitionSpec as P

NX, NY, NZ = 4, 4, 8
TOK = 256
DIM = 128
GROUP = 4
BACK = 2
ROWS = NY + BACK
SLOTS = ROWS * NZ
SLOT_ROWS = 2 * TOK + 16
LANES = GROUP * TOK
NEG = -1e30
FAR_ID = 512.0
SCALE = 1.4426950408889634 * DIM ** -0.5


def place():
    me = lax.axis_index("ctx")
    return me, me // (NY * NZ), (me // NZ) % NY, me % NZ


def index_of(x, y, z):
    return (x * NY + y) * NZ + z


def remote(src, dst, send, recv, device):
    return pltpu.make_async_remote_copy(src_ref=src, dst_ref=dst, send_sem=send, recv_sem=recv,
                                        device_id=device, device_id_type=pl.DeviceIdType.MESH)


def attention_kernel(q_ref, k_ref, v_ref, seg_ref, out_ref, q_buf, v_buf, seg_buf, vt_buf, qt_buf,
                     kv, qt, qe, acc, peak, first, lead, o_buf, load_sem,
                     y_send, y_recv, q_send, q_recv, z_send, z_recv, x_send, x_recv, o_send, o_recv):
    me, x, y, z = place()
    core = lax.axis_index("kvh")
    half = NZ // 2

    def dev(x_, y_, z_):
        return (index_of(x_, y_, z_), core)

    y_peers = [lax.rem(y + d, NY) for d in range(1, NY)]
    z_next, z_prev = lax.rem(z + 1, NZ), lax.rem(z + NZ - 1, NZ)
    x_next, x_prev = lax.rem(x + 1, NX), lax.rem(x + NX - 1, NX)
    barrier = pltpu.get_barrier_semaphore()
    friends = ([dev(x, p, z) for p in y_peers] + [(index_of(x, p, z), 1 - core) for p in [y] + y_peers]
               + [dev(x, y, z_next), dev(x, y, z_prev), dev(x_next, y, z), dev(x_prev, y, z)])
    for friend in friends:
        pl.semaphore_signal(barrier, inc=1, device_id=friend, device_id_type=pl.DeviceIdType.MESH)
    load_v = pltpu.make_async_copy(v_ref, v_buf, load_sem.at[0])
    load_q = pltpu.make_async_copy(q_ref, q_buf, load_sem.at[1])
    load_v.start()
    load_q.start()

    @pl.when(x == 0)
    def _():
        def blank(at, _):
            kv[at, :2 * TOK, :] = jnp.zeros((2 * TOK, DIM), jnp.bfloat16)
            kv[at, 2 * TOK:, :] = jnp.full((16, DIM), -1.0, jnp.bfloat16)
            return 0

        lax.fori_loop(0, BACK * NZ, blank, 0)

    ids = seg_ref[...].astype(jnp.float32)
    line = lax.broadcasted_iota(jnp.int32, (16, 128), 0)
    ids = jnp.where(line == 0, ids[0:1], jnp.where(line == 1, ids[1:2], FAR_ID))
    seg_buf[...] = ids.astype(jnp.bfloat16)
    load_v.wait()
    for p in range(NY):
        turned = v_buf[:, p * DIM:(p + 1) * DIM].T
        vt_buf[p, :DIM, :] = turned[:, :DIM]
        vt_buf[p, DIM:, :] = turned[:, DIM:]
    pl.semaphore_wait(barrier, len(friends))

    def slot(row, shift):
        return (BACK + row) * NZ + lax.rem(z + shift + NZ, NZ)

    def head_cols(p):
        return pl.ds(pl.multiple_of(p * DIM, DIM), DIM)

    mine = (BACK + y) * NZ + z
    sent = []
    for n, p in enumerate(y_peers):
        for i, (src, lo, rows) in enumerate(((k_ref.at[:, head_cols(p)], 0, TOK), (vt_buf.at[p], TOK, TOK),
                                             (seg_buf, 2 * TOK, 16))):
            copy = remote(src, kv.at[mine, pl.ds(lo, rows)], y_send.at[n, i], y_recv.at[y], dev(x, p, z))
            copy.start()
            sent.append(copy)
    pltpu.make_async_copy(k_ref.at[:, head_cols(y)], kv.at[mine, pl.ds(0, TOK)], y_recv.at[y]).start()
    pltpu.make_async_copy(vt_buf.at[y], kv.at[mine, pl.ds(TOK, TOK)], y_recv.at[y]).start()
    pltpu.make_async_copy(seg_buf, kv.at[mine, pl.ds(2 * TOK, 16)], y_recv.at[y]).start()
    load_q.wait()
    for p in range(NY):
        for g in range(GROUP):
            h = p * GROUP + g
            qt_buf[p, :, g * TOK:(g + 1) * TOK] = q_buf[:, h * DIM:(h + 1) * DIM].T

    def shift_of(way, step):
        return step * (2 * way - 1)

    def z_copy(way, row, step):
        at = kv.at[slot(row, shift_of(way, step - 1))]
        neighbour = jnp.where(way == 0, z_next, z_prev)
        return remote(at, at, z_send.at[way, row, step - 1], z_recv.at[way, row, step - 1], dev(x, y, neighbour))

    def x_copy(row, way, step):
        shift = shift_of(way, step)
        return remote(kv.at[slot(row, shift)], kv.at[slot(row - NY, shift)], x_send.at[row - NY + BACK, way, step],
                      x_recv.at[row - NY + BACK, way, step], dev(x_next, y, z))

    def last_way(row):
        return lax.rem(row + 1, 2)

    def pass_on(way, row, step):
        @pl.when((step < half - 1) | ((step == half - 1) & (way == last_way(row))))
        def _():
            z_copy(way, row, step + 1).start()

        @pl.when((row >= NY - BACK) & (x < NX - 1))
        def _():
            x_copy(row, way, step).start()

    for row in (3, 2, 1, 0):
        at = kv.at[slot(row, 0)]
        pltpu.make_async_copy(at, at, y_recv.at[row]).wait()
        z_copy(0, row, 1).start()
        z_copy(1, row, 1).start()
        if row >= NY - BACK:
            @pl.when(x < NX - 1)
            def _():
                x_copy(row, 0, 0).start()
    asked = []
    for n, p in enumerate(y_peers):
        copy = remote(qt_buf.at[p], qt.at[y], q_send.at[n], q_recv.at[n], dev(x, p, z))
        copy.start()
        asked.append(copy)
    own_q = pltpu.make_async_copy(qt_buf.at[y], qt.at[y], q_send.at[NY - 1])
    own_q.start()

    def first_step(j, _):
        row, way = NY - 1 - j // 2, j % 2
        z_copy(way, row, 1).wait_recv()
        pass_on(way, row, 1)
        return 0

    lax.fori_loop(0, 2 * NY, first_step, 0)
    for copy in asked:
        copy.wait_recv()
    own_q.wait()

    def spread(b, _):
        scaled = qt[b].astype(jnp.float32) * SCALE
        high = scaled.astype(jnp.bfloat16)
        qe[b, :DIM, :] = high
        qe[b, DIM:, :] = (scaled - high.astype(jnp.float32)).astype(jnp.bfloat16)
        return 0

    lax.fori_loop(0, NY, spread, 0)
    key = lax.broadcasted_iota(jnp.int32, (TOK, TOK), 0)
    token = lax.broadcasted_iota(jnp.int32, (TOK, TOK), 1)

    def block_of(at):
        k = kv[at, :TOK, :]
        return jnp.concatenate([k, k], axis=1), [kv[at, TOK:TOK + DIM, :], kv[at, TOK + DIM:2 * TOK, :]]

    def bias_of(at, b):
        there = kv[at, 2 * TOK:, :].astype(jnp.float32)
        less = jnp.where(there < first[b, 0:1, :], 1.0, 0.0)
        count = jnp.sum(jnp.sum(less, axis=0, keepdims=True), axis=1, keepdims=True)
        bound = (lead[b, 0:1, :] + count).astype(jnp.int32)
        return jnp.where(key >= bound, 0.0, NEG)

    def chains(jobs):
        todo = []
        for b, slots, biases, going in jobs:
            loaded = [block_of(at) for at in slots]
            vt = jnp.concatenate([part for _, parts in loaded for part in parts], axis=1)
            vt = jnp.concatenate([vt, jnp.ones((16, vt.shape[1]), jnp.bfloat16)], axis=0)
            for g in range(GROUP):
                todo.append((b, slice(g * TOK, (g + 1) * TOK), [k for k, _ in loaded], biases, vt, going))
        count = len(todo)
        scores, weights = [None] * count, [None] * count
        for i in range(count + 2):
            if i < count:
                b, cols, ks, biases, _, _ = todo[i]
                q = qe[b, :, cols]
                scores[i] = [jnp.dot(k, q, preferred_element_type=jnp.float32) for k in ks]
            if 0 <= i - 1 < count:
                b, cols, _, biases, _, going = todo[i - 1]
                t = [one + bias for one, bias in zip(scores[i - 1], biases)]
                top = t[0]
                for one in t[1:]:
                    top = jnp.maximum(top, one)
                new = jnp.max(top, axis=0, keepdims=True)
                fade = None
                if going:
                    old = peak[b, 0:1, cols]
                    new = jnp.maximum(old, new)
                    fade = jnp.exp2(old - new)
                peak[b, 0:1, cols] = new
                w = jnp.concatenate([jnp.exp2(one - new).astype(jnp.bfloat16) for one in t], axis=0)
                scores[i - 1] = None
                weights[i - 1] = (w, fade)
            if i >= 2:
                b, cols, _, _, vt, going = todo[i - 2]
                w, fade = weights[i - 2]
                o = jnp.dot(vt, w, preferred_element_type=jnp.float32)
                acc[b, :, cols] = acc[b, :, cols] * fade + o if going else o
                weights[i - 2] = None

    def wait_x(row, way, step):
        @pl.when(x > 0)
        def _():
            x_copy(row, way, step).wait_recv()

    for row in (NY - 1, NY - 2):
        wait_x(row, 0, 0)

    def own_work(j, _):
        b = NY - 1 - j
        at = slot(b, 0)
        own = kv[at, 2 * TOK:, :].astype(jnp.float32)
        row = jnp.concatenate([own[0:1], own[1:2]], axis=1)
        rows = jnp.broadcast_to(row, (TOK, TOK))
        begin = row[:, 0:1]
        first[b] = jnp.broadcast_to(begin, (8, 128))
        lead[b] = jnp.broadcast_to(jnp.where(row == begin, 0.0, 4096.0), (8, TOK))
        allowed = (rows == rows.T) & (key <= token)
        slots = [at, slot(b - 1, 0), slot(b - 2, 0)]
        chains([(b, slots, [jnp.where(allowed, 0.0, NEG)] + [bias_of(one, b) for one in slots[1:]], False)])
        return 0

    lax.fori_loop(0, NY, own_work, 0)

    def pair_work(pair, way, step):
        shift = shift_of(way, step)
        there = lax.rem(z + shift + NZ, NZ)
        jobs = []
        for i in (1, 0):
            b = 2 * pair + i
            slots = [slot(b - 1, shift), slot(jnp.where(there < z, b, b - 2), shift)]
            jobs.append((b, slots, [bias_of(at, b) for at in slots], True))
        chains(jobs)

    def later_step(step, _):
        def arrive(j, _):
            row, way = NY - 1 - j // 2, j % 2

            @pl.when((step < half) | (way == last_way(row)))
            def _():
                z_copy(way, row, step).wait_recv()
                pass_on(way, row, step)
            return 0

        lax.fori_loop(0, 2 * NY, arrive, 0)

        def catch_up(j, _):
            @pl.when(j >= 2)
            def _():
                for row in (NY - 1, NY - 2):
                    wait_x(row, j % 2, step - 1)
            pair_work(1 - j // 2, j % 2, step - 1)
            return 0

        lax.fori_loop(0, 4, catch_up, 0)
        return 0

    lax.fori_loop(2, half + 1, later_step, 0)

    rows = TOK // 2
    wide = GROUP * DIM
    cols = out_ref.at[:, pl.ds(pl.multiple_of((core * NY + y) * wide, wide), wide)]

    def part(b, c):
        return o_buf.at[b, pl.ds(pl.multiple_of(c * rows, rows), rows)]

    def over(b):
        return remote(part(b, 1 - core), cols, o_send.at[b, 1], o_recv.at[y, 1], (index_of(x, b, z), 1 - core))

    def along(b):
        return remote(part(b, core), cols, o_send.at[b, 0], o_recv.at[y, 0], (index_of(x, b, z), core))

    def stay(b):
        return pltpu.make_async_copy(part(b, core), cols, o_recv.at[y, 0])

    def send_back(b):
        mixed = acc[b, :DIM, :] / acc[b, DIM:DIM + 1, :]
        for g in range(GROUP):
            o_buf[b, :, g * DIM:(g + 1) * DIM] = mixed[:, g * TOK:(g + 1) * TOK].T.astype(jnp.bfloat16)
        over(b).start()

        @pl.when(b != y)
        def _():
            along(b).start()

        @pl.when(b == y)
        def _():
            stay(b).start()

    def finish(j, _):
        @pl.when(j == 1)
        def _():
            for row in (NY - 1, NY - 2):
                wait_x(row, last_way(row), half)
        pair_work(1 - j, 0, half)
        for i in (1, 0):
            send_back(2 * (1 - j) + i)
        return 0

    lax.fori_loop(0, 2, finish, 0)

    for copy in sent + asked:
        copy.wait_send()

    def z_drain(j, _):
        row, way, step = j // (2 * half), (j // half) % 2, 1 + j % half

        @pl.when((step < half) | (way == last_way(row)))
        def _():
            z_copy(way, row, step).wait_send()
        return 0

    lax.fori_loop(0, 2 * NY * half, z_drain, 0)

    def x_drain(j, _):
        row, way, step = NY - 1 - j // (2 * (half + 1)), (j // (half + 1)) % 2, j % (half + 1)
        sent_one = jnp.where(step == 0, way == 0, (step < half) | (way == last_way(row)))

        @pl.when(sent_one & (x < NX - 1))
        def _():
            x_copy(row, way, step).wait_send()
        return 0

    lax.fori_loop(0, 2 * BACK * (half + 1), x_drain, 0)
    for b in range(NY):
        over(b).wait_send()

        @pl.when(b != y)
        def _():
            along(b).wait_send()
        for e in range(2):
            pltpu.make_async_copy(part(b, core), cols, o_recv.at[b, e]).wait()


def per_device(queries, keys, values, segment_ids):
    any_spec = pl.BlockSpec(memory_space=pl.ANY)
    vmem_spec = pl.BlockSpec(memory_space=pltpu.VMEM)
    dma = pltpu.SemaphoreType.DMA
    bf16, f32 = jnp.bfloat16, jnp.float32
    half = NZ // 2
    return pl.pallas_call(
        attention_kernel,
        out_shape=jax.ShapeDtypeStruct((TOK // 2, 2 * NY * GROUP * DIM), bf16),
        in_specs=[any_spec, any_spec, any_spec, vmem_spec],
        out_specs=any_spec,
        scratch_shapes=[
            pltpu.VMEM(queries.shape, bf16), pltpu.VMEM(values.shape, bf16), pltpu.VMEM((16, 128), bf16),
            pltpu.VMEM((NY, 2 * DIM, TOK // 2), bf16), pltpu.VMEM((NY, DIM, LANES), bf16),
            pltpu.VMEM((SLOTS, SLOT_ROWS, DIM), bf16), pltpu.VMEM((NY, DIM, LANES), bf16),
            pltpu.VMEM((NY, 2 * DIM, LANES), bf16), pltpu.VMEM((NY, DIM + 16, LANES), f32), pltpu.VMEM((NY, 8, LANES), f32),
            pltpu.VMEM((NY, 8, 128), f32), pltpu.VMEM((NY, 8, TOK), f32), pltpu.VMEM((NY, TOK, GROUP * DIM), bf16),
            dma((2,)), dma((NY - 1, 3)), dma((NY,)), dma((NY,)), dma((NY - 1,)),
            dma((2, NY, half)), dma((2, NY, half)), dma((BACK, 2, half + 1)), dma((BACK, 2, half + 1)),
            dma((NY, 2)), dma((NY, 2))],
        compiler_params=pltpu.CompilerParams(collective_id=0, has_side_effects=True,
                                             vmem_limit_bytes=60 * 1024 * 1024),
        name="attention",
    )(queries, keys, values, segment_ids.reshape(2, 128))


def solution(mesh):
    return jax.shard_map(
        per_device,
        mesh=mesh,
        in_specs=(P("ctx", "kvh"), P("ctx", "kvh"), P("ctx", "kvh"), P("ctx")),
        out_specs=P(("ctx", "kvh"), None),
        check_vma=False,
    )
```

time: 416 us -> 86 us (0.21)
  waiting for transfers between devices: 242 us -> 0 us
  Pallas kernels: 0 us -> 83.5 us
  matrix products: 66 us -> 0 us
  starting transfers between devices: 53.8 us -> 0 us
  local copies, waits for them, and re-layouts: 25.4 us -> 2.29 us
  other arithmetic: 20.6 us -> 0 us
  blocking collectives: 4.58 us -> 0 us
    ppermute x21 -> x0, waiting for transfers between devices: 242 us -> none  [passed_along(): return lax.ppermute(value, axis, pairs)]
    pallas_call x0 -> x1, Pallas kernels: none -> 83.5 us  [per_device(): pl.pallas_call(attention_kernel, out_shape=jax.ShapeDtypeStruct((TOK // 2...]
    dot_general x34 -> x0, matrix products: 66 us -> none  [the longest x17 34.1 us: compute_tile(): jnp.einsum('tgqd,sgd->tgqs', q_heads, k_heads, preferred_element_type=jnp...]
    ppermute x21 -> x0, starting transfers between devices: 53.8 us -> none  [passed_along(): return lax.ppermute(value, axis, pairs)]
    reduce_sum x17 -> x0, other arithmetic: 15 us -> none  [compute_tile(): denom_sum = denom_sum * fading + jnp.sum(weights_p, axis=-1)]
    while x32 -> x0, local copies, waits for them, and re-layouts: 12.8 us -> none
    all_to_all x1 -> x0, blocking collectives: 4.58 us -> none  [per_device(): return lax.all_to_all(mixed, 'kvh', split_axis=0, concat_axis=1, tiled=True)]
    unnamed x12 -> x1, local copies, waits for them, and re-layouts: 6.63 us -> 2.29 us
  transfers between devices with their start and end apart: 21 -> 0, of which waited for: 20 -> 0; matrix products, arithmetic and copies ran while one was open for 4% -> 0% of each run, Pallas kernels for 0% -> 0%
where the time goes in v1:
time: 86 us; the launch traced here: 85.8 us
  Pallas kernels  83.5 us (97%)
  local copies, waits for them, and re-layouts  2.29 us (3%)
    pallas_call x1, Pallas kernels, per_device(): pl.pallas_call(attention_kernel, out_shape=jax.ShapeDtypeStruct((TOK // 2...  83.5 us
    unnamed x1, local copies, waits for them, and re-layouts  2.29 us

profile of v1, /device:TPU:6, one launch (start us, length us, event | category | flops | bytes accessed | tf_op | source)
XLA Modules:
  0.0 85.8 jit_solution(16002609377327933193)
XLA Ops:
  0.0 83.5 %attention.1 = bf16[128,4096]{1,0:T(8,128)(2,1)} custom-call(bf16[256,2048]{1,0:T(8,128)(2,1)} %q_ref.1, bf16[256,512]{1,0:T(8,128)(2,1)} %k_ref.1, bf16[256,512]{1,0:T(8,128)(2,1)} %v_ref.1, s32[2,128]{1,0:T(2,128)} %bitcast.1), custom_call_target="tpu_custom_call" | custom-call | tf_op jit(solution)/shard_map/attention/pallas_call | solution.py:355
  83.5 2.3 %copy.6 = bf16[128,4096]{1,0:T(8,128)(2,1)} copy(bf16[128,4096]{1,0:T(8,128)(2,1)} %attention.1) | data formatting | bytes 2097152

commit v2 on v1

--- a/solution.py
+++ b/solution.py
@@ -34,7 +34,7 @@
 
 
 def attention_kernel(q_ref, k_ref, v_ref, seg_ref, out_ref, q_buf, v_buf, seg_buf, vt_buf, qt_buf,
-                     kv, qt, qe, acc, peak, first, lead, o_buf, load_sem,
+                     kv, qe, acc, peak, first, o_buf, load_sem,
                      y_send, y_recv, q_send, q_recv, z_send, z_recv, x_send, x_recv, o_send, o_recv):
     me, x, y, z = place()
     core = lax.axis_index("kvh")
@@ -135,10 +135,10 @@
                 x_copy(row, 0, 0).start()
     asked = []
     for n, p in enumerate(y_peers):
-        copy = remote(qt_buf.at[p], qt.at[y], q_send.at[n], q_recv.at[n], dev(x, p, z))
+        copy = remote(qt_buf.at[p], qe.at[y, pl.ds(0, DIM)], q_send.at[n], q_recv.at[n], dev(x, p, z))
         copy.start()
         asked.append(copy)
-    own_q = pltpu.make_async_copy(qt_buf.at[y], qt.at[y], q_send.at[NY - 1])
+    own_q = pltpu.make_async_copy(qt_buf.at[y], qe.at[y, pl.ds(0, DIM)], q_send.at[NY - 1])
     own_q.start()
 
     def first_step(j, _):
@@ -152,65 +152,57 @@
         copy.wait_recv()
     own_q.wait()
 
-    def spread(b, _):
-        scaled = qt[b].astype(jnp.float32) * SCALE
-        high = scaled.astype(jnp.bfloat16)
-        qe[b, :DIM, :] = high
-        qe[b, DIM:, :] = (scaled - high.astype(jnp.float32)).astype(jnp.bfloat16)
-        return 0
-
-    lax.fori_loop(0, NY, spread, 0)
     key = lax.broadcasted_iota(jnp.int32, (TOK, TOK), 0)
     token = lax.broadcasted_iota(jnp.int32, (TOK, TOK), 1)
 
-    def block_of(at):
-        k = kv[at, :TOK, :]
-        return jnp.concatenate([k, k], axis=1), [kv[at, TOK:TOK + DIM, :], kv[at, TOK + DIM:2 * TOK, :]]
-
-    def bias_of(at, b):
+    lane = lax.broadcasted_iota(jnp.int32, (TOK, DIM), 1)
+    line = lax.broadcasted_iota(jnp.int32, (TOK, DIM), 0)
+    plain = jnp.where(lane == 1, 1.0, 0.0)
+
+    def early_keys(at, b):
         there = kv[at, 2 * TOK:, :].astype(jnp.float32)
         less = jnp.where(there < first[b, 0:1, :], 1.0, 0.0)
-        count = jnp.sum(jnp.sum(less, axis=0, keepdims=True), axis=1, keepdims=True)
-        bound = (lead[b, 0:1, :] + count).astype(jnp.int32)
-        return jnp.where(key >= bound, 0.0, NEG)
+        count = jnp.sum(jnp.sum(less, axis=0, keepdims=True), axis=1, keepdims=True).astype(jnp.int32)
+        extra = jnp.where((lane == 0) & (line < count), NEG, plain).astype(jnp.bfloat16)
+        return jnp.concatenate([kv[at, :TOK, :], extra], axis=1)
+
+    def own_keys(at):
+        return jnp.concatenate([kv[at, :TOK, :], jnp.zeros((TOK, DIM), jnp.bfloat16)], axis=1)
+
+    def turned_values(slots):
+        vt = jnp.concatenate([kv[at, lo:lo + DIM, :] for at in slots for lo in (TOK, TOK + DIM)], axis=1)
+        return jnp.concatenate([vt, jnp.ones((16, vt.shape[1]), jnp.bfloat16)], axis=0)
 
     def chains(jobs):
-        todo = []
-        for b, slots, biases, going in jobs:
-            loaded = [block_of(at) for at in slots]
-            vt = jnp.concatenate([part for _, parts in loaded for part in parts], axis=1)
-            vt = jnp.concatenate([vt, jnp.ones((16, vt.shape[1]), jnp.bfloat16)], axis=0)
-            for g in range(GROUP):
-                todo.append((b, slice(g * TOK, (g + 1) * TOK), [k for k, _ in loaded], biases, vt, going))
+        todo = [(b, slice(g * TOK, (g + 1) * TOK), keys, vt, bias, going)
+                for b, keys, vt, bias, going in jobs for g in range(GROUP)]
         count = len(todo)
-        scores, weights = [None] * count, [None] * count
+        scores, weights, done = [None] * count, [None] * count, []
         for i in range(count + 2):
             if i < count:
-                b, cols, ks, biases, _, _ = todo[i]
-                q = qe[b, :, cols]
-                scores[i] = [jnp.dot(k, q, preferred_element_type=jnp.float32) for k in ks]
+                b, cols, keys, _, _, _ = todo[i]
+                scores[i] = jnp.dot(keys, qe[b, :, cols], preferred_element_type=jnp.float32)
             if 0 <= i - 1 < count:
-                b, cols, _, biases, _, going = todo[i - 1]
-                t = [one + bias for one, bias in zip(scores[i - 1], biases)]
-                top = t[0]
-                for one in t[1:]:
-                    top = jnp.maximum(top, one)
-                new = jnp.max(top, axis=0, keepdims=True)
+                b, cols, _, _, bias, going = todo[i - 1]
+                s = scores[i - 1]
+                if bias is not None:
+                    s = jnp.concatenate([s[:TOK] + bias, s[TOK:]], axis=0)
+                new = jnp.max(s, axis=0, keepdims=True)
                 fade = None
                 if going:
                     old = peak[b, 0:1, cols]
                     new = jnp.maximum(old, new)
-                    fade = jnp.exp2(old - new)
-                peak[b, 0:1, cols] = new
-                w = jnp.concatenate([jnp.exp2(one - new).astype(jnp.bfloat16) for one in t], axis=0)
+                    fade = jnp.exp2((old - new) * SCALE)
+                weights[i - 1] = (jnp.exp2((s - new) * SCALE).astype(jnp.bfloat16), new, fade)
                 scores[i - 1] = None
-                weights[i - 1] = (w, fade)
             if i >= 2:
-                b, cols, _, _, vt, going = todo[i - 2]
-                w, fade = weights[i - 2]
-                o = jnp.dot(vt, w, preferred_element_type=jnp.float32)
-                acc[b, :, cols] = acc[b, :, cols] * fade + o if going else o
+                b, cols, _, vt, _, going = todo[i - 2]
+                w, new, fade = weights[i - 2]
+                done.append((b, cols, new, fade, jnp.dot(vt, w, preferred_element_type=jnp.float32)))
                 weights[i - 2] = None
+        for b, cols, new, fade, o in done:
+            peak[b, 0:1, cols] = new
+            acc[b, :, cols] = o if fade is None else acc[b, :, cols] * fade + o
 
     def wait_x(row, way, step):
         @pl.when(x > 0)
@@ -221,20 +213,26 @@
         wait_x(row, 0, 0)
 
     def own_work(j, _):
-        b = NY - 1 - j
-        at = slot(b, 0)
-        own = kv[at, 2 * TOK:, :].astype(jnp.float32)
-        row = jnp.concatenate([own[0:1], own[1:2]], axis=1)
-        rows = jnp.broadcast_to(row, (TOK, TOK))
-        begin = row[:, 0:1]
-        first[b] = jnp.broadcast_to(begin, (8, 128))
-        lead[b] = jnp.broadcast_to(jnp.where(row == begin, 0.0, 4096.0), (8, TOK))
-        allowed = (rows == rows.T) & (key <= token)
-        slots = [at, slot(b - 1, 0), slot(b - 2, 0)]
-        chains([(b, slots, [jnp.where(allowed, 0.0, NEG)] + [bias_of(one, b) for one in slots[1:]], False)])
-        return 0
-
-    lax.fori_loop(0, NY, own_work, 0)
+        jobs = []
+        for i in (1, 0):
+            b = NY - 2 - 2 * j + i
+            at = slot(b, 0)
+            own = kv[at, 2 * TOK:, :].astype(jnp.float32)
+            row = jnp.concatenate([own[0:1], own[1:2]], axis=1)
+            rows = jnp.broadcast_to(row, (TOK, TOK))
+            begin = row[:, 0:1]
+            first[b] = jnp.broadcast_to(begin, (8, 128))
+            rest = jnp.concatenate([jnp.where(row == begin, 0.0, NEG)] * GROUP, axis=1)
+            which = lax.broadcasted_iota(jnp.int32, (DIM, LANES), 0)
+            qe[b, DIM:, :] = jnp.where(which == 0, 1.0, jnp.where(which == 1, rest, 0.0)).astype(jnp.bfloat16)
+            bias = jnp.where((rows == rows.T) & (key <= token), 0.0, NEG)
+            early = [slot(b - 1, 0), slot(b - 2, 0)]
+            keys = jnp.concatenate([own_keys(at)] + [early_keys(one, b) for one in early], axis=0)
+            jobs.append((b, keys, turned_values([at] + early), bias, False))
+        chains(jobs)
+        return 0
+
+    lax.fori_loop(0, NY // 2, own_work, 0)
 
     def pair_work(pair, way, step):
         shift = shift_of(way, step)
@@ -243,7 +241,8 @@
         for i in (1, 0):
             b = 2 * pair + i
             slots = [slot(b - 1, shift), slot(jnp.where(there < z, b, b - 2), shift)]
-            jobs.append((b, slots, [bias_of(at, b) for at in slots], True))
+            keys = jnp.concatenate([early_keys(at, b) for at in slots], axis=0)
+            jobs.append((b, keys, turned_values(slots), None, True))
         chains(jobs)
 
     def later_step(step, _):
@@ -360,9 +359,9 @@
         scratch_shapes=[
             pltpu.VMEM(queries.shape, bf16), pltpu.VMEM(values.shape, bf16), pltpu.VMEM((16, 128), bf16),
             pltpu.VMEM((NY, 2 * DIM, TOK // 2), bf16), pltpu.VMEM((NY, DIM, LANES), bf16),
-            pltpu.VMEM((SLOTS, SLOT_ROWS, DIM), bf16), pltpu.VMEM((NY, DIM, LANES), bf16),
+            pltpu.VMEM((SLOTS, SLOT_ROWS, DIM), bf16),
             pltpu.VMEM((NY, 2 * DIM, LANES), bf16), pltpu.VMEM((NY, DIM + 16, LANES), f32), pltpu.VMEM((NY, 8, LANES), f32),
-            pltpu.VMEM((NY, 8, 128), f32), pltpu.VMEM((NY, 8, TOK), f32), pltpu.VMEM((NY, TOK, GROUP * DIM), bf16),
+            pltpu.VMEM((NY, 8, 128), f32), pltpu.VMEM((NY, TOK, GROUP * DIM), bf16),
             dma((2,)), dma((NY - 1, 3)), dma((NY,)), dma((NY,)), dma((NY - 1,)),
             dma((2, NY, half)), dma((2, NY, half)), dma((BACK, 2, half + 1)), dma((BACK, 2, half + 1)),
             dma((NY, 2)), dma((NY, 2))],

time: 86 us -> 86.7 us (level)
  no operation moved by 1% of the time
where the time goes in v2:
time: 86.7 us; the launch traced here: 86.5 us
  Pallas kernels  84.2 us (97%)
  local copies, waits for them, and re-layouts  2.29 us (3%)
    pallas_call x1, Pallas kernels, per_device(): pl.pallas_call(attention_kernel, out_shape=jax.ShapeDtypeStruct((TOK // 2...  84.2 us
    unnamed x1, local copies, waits for them, and re-layouts  2.29 us

profile of v2, /device:TPU:6, one launch (start us, length us, event | category | flops | bytes accessed | tf_op | source)
XLA Modules:
  0.0 86.5 jit_solution(3656776170777804188)
XLA Ops:
  0.0 84.2 %attention.1 = bf16[128,4096]{1,0:T(8,128)(2,1)} custom-call(bf16[256,2048]{1,0:T(8,128)(2,1)} %q_ref.1, bf16[256,512]{1,0:T(8,128)(2,1)} %k_ref.1, bf16[256,512]{1,0:T(8,128)(2,1)} %v_ref.1, s32[2,128]{1,0:T(2,128)} %bitcast.1), custom_call_target="tpu_custom_call" | custom-call | tf_op jit(solution)/shard_map/attention/pallas_call | solution.py:354
  84.3 2.3 %copy.6 = bf16[128,4096]{1,0:T(8,128)(2,1)} copy(bf16[128,4096]{1,0:T(8,128)(2,1)} %attention.1) | data formatting | bytes 2097152

commit v3 on v2

--- a/solution.py
+++ b/solution.py
@@ -33,9 +33,10 @@
                                         device_id=device, device_id_type=pl.DeviceIdType.MESH)
 
 
-def attention_kernel(q_ref, k_ref, v_ref, seg_ref, out_ref, q_buf, v_buf, seg_buf, vt_buf, qt_buf,
+def attention_kernel(q_ref, k_ref, v_ref, seg_ref, out_ref, q_buf, v_buf, seg_in, seg_buf, vt_buf, qt_buf,
                      kv, qe, acc, peak, first, o_buf, load_sem,
-                     y_send, y_recv, q_send, q_recv, z_send, z_recv, x_send, x_recv, o_send, o_recv):
+                     y_send, y_recv, q_send, q_recv, z_send, z_recv, x_send, x_recv,
+                     side_send, side_recv, o_send, o_recv):
     me, x, y, z = place()
     core = lax.axis_index("kvh")
     half = NZ // 2
@@ -53,36 +54,32 @@
         pl.semaphore_signal(barrier, inc=1, device_id=friend, device_id_type=pl.DeviceIdType.MESH)
     load_v = pltpu.make_async_copy(v_ref, v_buf, load_sem.at[0])
     load_q = pltpu.make_async_copy(q_ref, q_buf, load_sem.at[1])
+    load_ids = pltpu.make_async_copy(seg_ref, seg_in, load_sem.at[2])
+    load_ids.start()
     load_v.start()
     load_q.start()
 
-    @pl.when(x == 0)
-    def _():
-        def blank(at, _):
-            kv[at, :2 * TOK, :] = jnp.zeros((2 * TOK, DIM), jnp.bfloat16)
-            kv[at, 2 * TOK:, :] = jnp.full((16, DIM), -1.0, jnp.bfloat16)
-            return 0
-
-        lax.fori_loop(0, BACK * NZ, blank, 0)
-
-    ids = seg_ref[...].astype(jnp.float32)
+    load_ids.wait()
+    ids = seg_in[...].astype(jnp.float32)
     line = lax.broadcasted_iota(jnp.int32, (16, 128), 0)
     ids = jnp.where(line == 0, ids[0:1], jnp.where(line == 1, ids[1:2], FAR_ID))
     seg_buf[...] = ids.astype(jnp.bfloat16)
+    def slot(row, shift):
+        return (BACK + row) * NZ + lax.rem(z + shift + NZ, NZ)
+
+    def head_cols(p):
+        return pl.ds(pl.multiple_of(p * DIM, DIM), DIM)
+
+    mine = (BACK + y) * NZ + z
+    pltpu.make_async_copy(k_ref.at[:, head_cols(y)], kv.at[mine, pl.ds(0, TOK)], y_recv.at[y]).start()
+    pltpu.make_async_copy(seg_buf, kv.at[mine, pl.ds(2 * TOK, 16)], y_recv.at[y]).start()
     load_v.wait()
     for p in range(NY):
         turned = v_buf[:, p * DIM:(p + 1) * DIM].T
         vt_buf[p, :DIM, :] = turned[:, :DIM]
         vt_buf[p, DIM:, :] = turned[:, DIM:]
+    pltpu.make_async_copy(vt_buf.at[y], kv.at[mine, pl.ds(TOK, TOK)], y_recv.at[y]).start()
     pl.semaphore_wait(barrier, len(friends))
-
-    def slot(row, shift):
-        return (BACK + row) * NZ + lax.rem(z + shift + NZ, NZ)
-
-    def head_cols(p):
-        return pl.ds(pl.multiple_of(p * DIM, DIM), DIM)
-
-    mine = (BACK + y) * NZ + z
     sent = []
     for n, p in enumerate(y_peers):
         for i, (src, lo, rows) in enumerate(((k_ref.at[:, head_cols(p)], 0, TOK), (vt_buf.at[p], TOK, TOK),
@@ -90,49 +87,68 @@
             copy = remote(src, kv.at[mine, pl.ds(lo, rows)], y_send.at[n, i], y_recv.at[y], dev(x, p, z))
             copy.start()
             sent.append(copy)
-    pltpu.make_async_copy(k_ref.at[:, head_cols(y)], kv.at[mine, pl.ds(0, TOK)], y_recv.at[y]).start()
-    pltpu.make_async_copy(vt_buf.at[y], kv.at[mine, pl.ds(TOK, TOK)], y_recv.at[y]).start()
-    pltpu.make_async_copy(seg_buf, kv.at[mine, pl.ds(2 * TOK, 16)], y_recv.at[y]).start()
+
+    def shift_of(way, step):
+        return step * (2 * way - 1)
+
+    def z_copy(way, row, step):
+        at = kv.at[slot(row, shift_of(way, step - 1))]
+        neighbour = jnp.where(way == 0, z_next, z_prev)
+        return remote(at, at, z_send.at[way, row, step - 1], z_recv.at[way, row, step - 1], dev(x, y, neighbour))
+
+    def x_copy(row, way, step):
+        shift = shift_of(way, step)
+        return remote(kv.at[slot(row, shift)], kv.at[slot(row - NY, shift)], x_send.at[row - NY + BACK, way, step],
+                      x_recv.at[row - NY + BACK, way, step], dev(x_next, y, z))
+
+    def last_way(row):
+        return lax.rem(row + 1, 2)
+
+    def row2_over_x(way, step):
+        return (lax.rem(z + shift_of(way, step) + NZ, NZ) >= z) & (step != 1)
+
+    def over_x(way, row, step):
+        return (row == NY - 1) | ((row == NY - 2) & row2_over_x(way, step))
+
+    def forward(way, row, step):
+        @pl.when(over_x(way, row, step) & (x < NX - 1))
+        def _():
+            x_copy(row, way, step).start()
+
+    def pass_on(way, row, step):
+        @pl.when((step < half - 1) | ((step == half - 1) & (way == last_way(row))))
+        def _():
+            z_copy(way, row, step + 1).start()
+        forward(way, row, step)
+
+    def side_copy(way):
+        at = kv.at[slot(-BACK, 0)]
+        return remote(at, at, side_send.at[way], side_recv.at[way], dev(x, y, z_prev if way else z_next))
+
+    def side_goes(way):
+        return (x > 0) & ((z >= 1) if way else (z == NZ - 1))
+
+    def side_comes(way):
+        return (x > 0) & ((z < NZ - 1) if way else (z == 0))
+
+    def row_of(i):
+        return lax.rem(y + jnp.where(i == 0, 0, jnp.where(i == 1, 1, jnp.where(i == 2, NY - 1, 2))), NY)
+
+    def first_sends(i, _):
+        row = row_of(i)
+        at = kv.at[slot(row, 0)]
+        pltpu.make_async_copy(at, at, y_recv.at[row]).wait()
+        z_copy(0, row, 1).start()
+        z_copy(1, row, 1).start()
+        forward(0, row, 0)
+        return 0
+
+    lax.fori_loop(0, NY, first_sends, 0)
     load_q.wait()
     for p in range(NY):
         for g in range(GROUP):
             h = p * GROUP + g
             qt_buf[p, :, g * TOK:(g + 1) * TOK] = q_buf[:, h * DIM:(h + 1) * DIM].T
-
-    def shift_of(way, step):
-        return step * (2 * way - 1)
-
-    def z_copy(way, row, step):
-        at = kv.at[slot(row, shift_of(way, step - 1))]
-        neighbour = jnp.where(way == 0, z_next, z_prev)
-        return remote(at, at, z_send.at[way, row, step - 1], z_recv.at[way, row, step - 1], dev(x, y, neighbour))
-
-    def x_copy(row, way, step):
-        shift = shift_of(way, step)
-        return remote(kv.at[slot(row, shift)], kv.at[slot(row - NY, shift)], x_send.at[row - NY + BACK, way, step],
-                      x_recv.at[row - NY + BACK, way, step], dev(x_next, y, z))
-
-    def last_way(row):
-        return lax.rem(row + 1, 2)
-
-    def pass_on(way, row, step):
-        @pl.when((step < half - 1) | ((step == half - 1) & (way == last_way(row))))
-        def _():
-            z_copy(way, row, step + 1).start()
-
-        @pl.when((row >= NY - BACK) & (x < NX - 1))
-        def _():
-            x_copy(row, way, step).start()
-
-    for row in (3, 2, 1, 0):
-        at = kv.at[slot(row, 0)]
-        pltpu.make_async_copy(at, at, y_recv.at[row]).wait()
-        z_copy(0, row, 1).start()
-        z_copy(1, row, 1).start()
-        if row >= NY - BACK:
-            @pl.when(x < NX - 1)
-            def _():
-                x_copy(row, 0, 0).start()
     asked = []
     for n, p in enumerate(y_peers):
         copy = remote(qt_buf.at[p], qe.at[y, pl.ds(0, DIM)], q_send.at[n], q_recv.at[n], dev(x, p, z))
@@ -141,13 +157,40 @@
     own_q = pltpu.make_async_copy(qt_buf.at[y], qe.at[y, pl.ds(0, DIM)], q_send.at[NY - 1])
     own_q.start()
 
-    def first_step(j, _):
-        row, way = NY - 1 - j // 2, j % 2
-        z_copy(way, row, 1).wait_recv()
-        pass_on(way, row, 1)
-        return 0
-
-    lax.fori_loop(0, 2 * NY, first_step, 0)
+    @pl.when(x == 0)
+    def _():
+        def blank(at, _):
+            kv[at, :2 * TOK, :] = jnp.zeros((2 * TOK, DIM), jnp.bfloat16)
+            kv[at, 2 * TOK:, :] = jnp.full((16, DIM), -1.0, jnp.bfloat16)
+            return 0
+
+        lax.fori_loop(0, BACK * NZ, blank, 0)
+
+    def arrive(step):
+        def one(j, _):
+            row, way = row_of(j // 2), j % 2
+
+            @pl.when((step < half) | (way == last_way(row)))
+            def _():
+                z_copy(way, row, step).wait_recv()
+                pass_on(way, row, step)
+            return 0
+
+        lax.fori_loop(0, 2 * NY, one, 0)
+
+    arrive(1)
+
+    def wait_x(row, way, step):
+        @pl.when(over_x(way, row, step) & (x > 0))
+        def _():
+            x_copy(row, way, step).wait_recv()
+
+    for row in (NY - 1, NY - 2):
+        wait_x(row, 0, 0)
+    for way in range(2):
+        @pl.when(side_goes(way))
+        def _():
+            side_copy(way).start()
     for copy in asked:
         copy.wait_recv()
     own_q.wait()
@@ -204,14 +247,6 @@
             peak[b, 0:1, cols] = new
             acc[b, :, cols] = o if fade is None else acc[b, :, cols] * fade + o
 
-    def wait_x(row, way, step):
-        @pl.when(x > 0)
-        def _():
-            x_copy(row, way, step).wait_recv()
-
-    for row in (NY - 1, NY - 2):
-        wait_x(row, 0, 0)
-
     def own_work(j, _):
         jobs = []
         for i in (1, 0):
@@ -246,29 +281,24 @@
         chains(jobs)
 
     def later_step(step, _):
-        def arrive(j, _):
-            row, way = NY - 1 - j // 2, j % 2
-
-            @pl.when((step < half) | (way == last_way(row)))
+        def catch_up(j, _):
+            @pl.when(j == 2)
             def _():
-                z_copy(way, row, step).wait_recv()
-                pass_on(way, row, step)
+                for way in range(2):
+                    for row in (NY - 1, NY - 2):
+                        wait_x(row, way, step)
+
+                    @pl.when((step == 1) & side_comes(way))
+                    def _():
+                        side_copy(way).wait_recv()
+            pair_work(1 - j // 2, j % 2, step)
             return 0
 
-        lax.fori_loop(0, 2 * NY, arrive, 0)
-
-        def catch_up(j, _):
-            @pl.when(j >= 2)
-            def _():
-                for row in (NY - 1, NY - 2):
-                    wait_x(row, j % 2, step - 1)
-            pair_work(1 - j // 2, j % 2, step - 1)
-            return 0
-
         lax.fori_loop(0, 4, catch_up, 0)
-        return 0
-
-    lax.fori_loop(2, half + 1, later_step, 0)
+        arrive(step + 1)
+        return 0
+
+    lax.fori_loop(1, half, later_step, 0)
 
     rows = TOK // 2
     wide = GROUP * DIM
@@ -327,14 +357,18 @@
 
     def x_drain(j, _):
         row, way, step = NY - 1 - j // (2 * (half + 1)), (j // (half + 1)) % 2, j % (half + 1)
-        sent_one = jnp.where(step == 0, way == 0, (step < half) | (way == last_way(row)))
-
-        @pl.when(sent_one & (x < NX - 1))
+        there_is = jnp.where(step == 0, way == 0, (step < half) | (way == last_way(row)))
+
+        @pl.when(there_is & over_x(way, row, step) & (x < NX - 1))
         def _():
             x_copy(row, way, step).wait_send()
         return 0
 
     lax.fori_loop(0, 2 * BACK * (half + 1), x_drain, 0)
+    for way in range(2):
+        @pl.when(side_goes(way))
+        def _():
+            side_copy(way).wait_send()
     for b in range(NY):
         over(b).wait_send()
 
@@ -347,28 +381,29 @@
 
 def per_device(queries, keys, values, segment_ids):
     any_spec = pl.BlockSpec(memory_space=pl.ANY)
-    vmem_spec = pl.BlockSpec(memory_space=pltpu.VMEM)
+    hbm_spec = pl.BlockSpec(memory_space=pltpu.HBM)
     dma = pltpu.SemaphoreType.DMA
     bf16, f32 = jnp.bfloat16, jnp.float32
     half = NZ // 2
     return pl.pallas_call(
         attention_kernel,
         out_shape=jax.ShapeDtypeStruct((TOK // 2, 2 * NY * GROUP * DIM), bf16),
-        in_specs=[any_spec, any_spec, any_spec, vmem_spec],
+        in_specs=[hbm_spec] * 4,
         out_specs=any_spec,
         scratch_shapes=[
-            pltpu.VMEM(queries.shape, bf16), pltpu.VMEM(values.shape, bf16), pltpu.VMEM((16, 128), bf16),
+            pltpu.VMEM(queries.shape, bf16), pltpu.VMEM(values.shape, bf16), pltpu.VMEM((2, 128), jnp.int32), pltpu.VMEM((16, 128), bf16),
             pltpu.VMEM((NY, 2 * DIM, TOK // 2), bf16), pltpu.VMEM((NY, DIM, LANES), bf16),
             pltpu.VMEM((SLOTS, SLOT_ROWS, DIM), bf16),
             pltpu.VMEM((NY, 2 * DIM, LANES), bf16), pltpu.VMEM((NY, DIM + 16, LANES), f32), pltpu.VMEM((NY, 8, LANES), f32),
             pltpu.VMEM((NY, 8, 128), f32), pltpu.VMEM((NY, TOK, GROUP * DIM), bf16),
-            dma((2,)), dma((NY - 1, 3)), dma((NY,)), dma((NY,)), dma((NY - 1,)),
+            dma((3,)), dma((NY - 1, 3)), dma((NY,)), dma((NY,)), dma((NY - 1,)),
             dma((2, NY, half)), dma((2, NY, half)), dma((BACK, 2, half + 1)), dma((BACK, 2, half + 1)),
-            dma((NY, 2)), dma((NY, 2))],
+            dma((2,)), dma((2,)), dma((NY, 2)), dma((NY, 2))],
         compiler_params=pltpu.CompilerParams(collective_id=0, has_side_effects=True,
-                                             vmem_limit_bytes=60 * 1024 * 1024),
+                                             vmem_limit_bytes=40 * 1024 * 1024),
         name="attention",
-    )(queries, keys, values, segment_ids.reshape(2, 128))
+    )(*(pltpu.with_memory_space_constraint(one, pltpu.HBM) for one in
+        (queries, keys, values, segment_ids.reshape(2, 128))))
 
 
 def solution(mesh):

time: 86.7 us -> 93.8 us (1.082)
  Pallas kernels: 84.2 us -> 92 us
  local copies, waits for them, and re-layouts: 2.29 us -> 0.97 us
    pallas_call x1, Pallas kernels: 84.2 us -> 92 us  [per_device(): pl.pallas_call(attention_kernel, out_shape=jax.ShapeDtypeStruct((TOK // 2...]
    unnamed x1, local copies, waits for them, and re-layouts: 2.29 us -> 0.97 us
where the time goes in v3:
time: 93.8 us; the launch traced here: 93 us
  Pallas kernels  92 us (98%)
  local copies, waits for them, and re-layouts  0.97 us (1%)
    pallas_call x1, Pallas kernels, per_device(): pl.pallas_call(attention_kernel, out_shape=jax.ShapeDtypeStruct((TOK // 2...  92 us

profile of v3, /device:TPU:6, one launch (start us, length us, event | category | flops | bytes accessed | tf_op | source)
XLA Modules:
  0.0 93.0 jit_solution(4118735816844799464)
XLA Ops:
  0.0 92.0 %attention.1 = bf16[128,4096]{1,0:T(8,128)(2,1)S(1)} custom-call(bf16[256,2048]{1,0:T(8,128)(2,1)} %q_ref.1, bf16[256,512]{1,0:T(8,128)(2,1)} %k_ref.1, bf16[256,512]{1,0:T(8,128)(2,1)} %v_ref.1, s32[2,128]{1,0:T(2,128)} %bitcast.1), custom_call_target="tpu_custom_call" | custom-call | tf_op jit(solution)/shard_map/attention/pallas_call | solution.py:388
  92.0 1.0 %copy.6 = bf16[128,4096]{1,0:T(8,128)(2,1)} copy(bf16[128,4096]{1,0:T(8,128)(2,1)S(1)} %attention.1) | data formatting | bytes 2097152

commit v4 on v3

--- a/solution.py
+++ b/solution.py
@@ -36,7 +36,7 @@
 def attention_kernel(q_ref, k_ref, v_ref, seg_ref, out_ref, q_buf, v_buf, seg_in, seg_buf, vt_buf, qt_buf,
                      kv, qe, acc, peak, first, o_buf, load_sem,
                      y_send, y_recv, q_send, q_recv, z_send, z_recv, x_send, x_recv,
-                     side_send, side_recv, o_send, o_recv):
+                     side_send, side_recv, ready, o_send, o_recv):
     me, x, y, z = place()
     core = lax.axis_index("kvh")
     half = NZ // 2
@@ -49,9 +49,13 @@
     x_next, x_prev = lax.rem(x + 1, NX), lax.rem(x + NX - 1, NX)
     barrier = pltpu.get_barrier_semaphore()
     friends = ([dev(x, p, z) for p in y_peers] + [(index_of(x, p, z), 1 - core) for p in [y] + y_peers]
-               + [dev(x, y, z_next), dev(x, y, z_prev), dev(x_next, y, z), dev(x_prev, y, z)])
+               + [dev(x, y, z_next), dev(x, y, z_prev)])
     for friend in friends:
         pl.semaphore_signal(barrier, inc=1, device_id=friend, device_id_type=pl.DeviceIdType.MESH)
+
+    @pl.when(x < NX - 1)
+    def _():
+        pl.semaphore_signal(barrier, inc=1, device_id=dev(x_next, y, z), device_id_type=pl.DeviceIdType.MESH)
     load_v = pltpu.make_async_copy(v_ref, v_buf, load_sem.at[0])
     load_q = pltpu.make_async_copy(q_ref, q_buf, load_sem.at[1])
     load_ids = pltpu.make_async_copy(seg_ref, seg_in, load_sem.at[2])
@@ -79,7 +83,12 @@
         vt_buf[p, :DIM, :] = turned[:, :DIM]
         vt_buf[p, DIM:, :] = turned[:, DIM:]
     pltpu.make_async_copy(vt_buf.at[y], kv.at[mine, pl.ds(TOK, TOK)], y_recv.at[y]).start()
-    pl.semaphore_wait(barrier, len(friends))
+    pl.semaphore_wait(barrier, len(friends) + jnp.where(x > 0, 1, 0))
+
+    @pl.when(x > 0)
+    def _():
+        pl.semaphore_signal(ready, inc=1, device_id=dev(x_prev, y, z), device_id_type=pl.DeviceIdType.MESH)
+
     sent = []
     for n, p in enumerate(y_peers):
         for i, (src, lo, rows) in enumerate(((k_ref.at[:, head_cols(p)], 0, TOK), (vt_buf.at[p], TOK, TOK),
@@ -140,10 +149,15 @@
         pltpu.make_async_copy(at, at, y_recv.at[row]).wait()
         z_copy(0, row, 1).start()
         z_copy(1, row, 1).start()
-        forward(0, row, 0)
         return 0
 
     lax.fori_loop(0, NY, first_sends, 0)
+
+    @pl.when(x < NX - 1)
+    def _():
+        pl.semaphore_wait(ready, 1)
+    forward(0, NY - 1, 0)
+    forward(0, NY - 2, 0)
     load_q.wait()
     for p in range(NY):
         for g in range(GROUP):
@@ -166,19 +180,19 @@
 
         lax.fori_loop(0, BACK * NZ, blank, 0)
 
-    def arrive(step):
-        def one(j, _):
-            row, way = row_of(j // 2), j % 2
-
+    def arrive(i, step):
+        row = row_of(i)
+        for way in range(2):
             @pl.when((step < half) | (way == last_way(row)))
             def _():
                 z_copy(way, row, step).wait_recv()
                 pass_on(way, row, step)
-            return 0
-
-        lax.fori_loop(0, 2 * NY, one, 0)
-
-    arrive(1)
+
+    def first_step(i, _):
+        arrive(i, 1)
+        return 0
+
+    lax.fori_loop(0, NY, first_step, 0)
 
     def wait_x(row, way, step):
         @pl.when(over_x(way, row, step) & (x > 0))
@@ -282,6 +296,10 @@
 
     def later_step(step, _):
         def catch_up(j, _):
+            @pl.when(step < half - 1)
+            def _():
+                arrive(j, step + 1)
+
             @pl.when(j == 2)
             def _():
                 for way in range(2):
@@ -295,10 +313,15 @@
             return 0
 
         lax.fori_loop(0, 4, catch_up, 0)
-        arrive(step + 1)
         return 0
 
     lax.fori_loop(1, half, later_step, 0)
+
+    def last_step(i, _):
+        arrive(i, half)
+        return 0
+
+    lax.fori_loop(0, NY, last_step, 0)
 
     rows = TOK // 2
     wide = GROUP * DIM
@@ -317,9 +340,9 @@
         return pltpu.make_async_copy(part(b, core), cols, o_recv.at[y, 0])
 
     def send_back(b):
-        mixed = acc[b, :DIM, :] / acc[b, DIM:DIM + 1, :]
+        mixed = (acc[b, :DIM, :] * (1.0 / acc[b, DIM:DIM + 1, :])).astype(jnp.bfloat16)
         for g in range(GROUP):
-            o_buf[b, :, g * DIM:(g + 1) * DIM] = mixed[:, g * TOK:(g + 1) * TOK].T.astype(jnp.bfloat16)
+            o_buf[b, :, g * DIM:(g + 1) * DIM] = mixed[:, g * TOK:(g + 1) * TOK].T
         over(b).start()
 
         @pl.when(b != y)
@@ -398,7 +421,7 @@
             pltpu.VMEM((NY, 8, 128), f32), pltpu.VMEM((NY, TOK, GROUP * DIM), bf16),
             dma((3,)), dma((NY - 1, 3)), dma((NY,)), dma((NY,)), dma((NY - 1,)),
             dma((2, NY, half)), dma((2, NY, half)), dma((BACK, 2, half + 1)), dma((BACK, 2, half + 1)),
-            dma((2,)), dma((2,)), dma((NY, 2)), dma((NY, 2))],
+            dma((2,)), dma((2,)), pltpu.SemaphoreType.REGULAR, dma((NY, 2)), dma((NY, 2))],
         compiler_params=pltpu.CompilerParams(collective_id=0, has_side_effects=True,
                                              vmem_limit_bytes=40 * 1024 * 1024),
         name="attention",

time: 93.8 us -> 84.7 us (0.903)
  Pallas kernels: 92 us -> 83.5 us
    pallas_call x1, Pallas kernels: 92 us -> 83.5 us  [per_device(): pl.pallas_call(attention_kernel, out_shape=jax.ShapeDtypeStruct((TOK // 2...]
where the time goes in v4:
time: 84.7 us; the launch traced here: 84.4 us
  Pallas kernels  83.5 us (99%)
  local copies, waits for them, and re-layouts  0.97 us (1%)
    pallas_call x1, Pallas kernels, per_device(): pl.pallas_call(attention_kernel, out_shape=jax.ShapeDtypeStruct((TOK // 2...  83.5 us

profile of v4, /device:TPU:6, one launch (start us, length us, event | category | flops | bytes accessed | tf_op | source)
XLA Modules:
  0.0 84.4 jit_solution(10141973057019671224)
XLA Ops:
  0.0 83.5 %attention.1 = bf16[128,4096]{1,0:T(8,128)(2,1)S(1)} custom-call(bf16[256,2048]{1,0:T(8,128)(2,1)} %q_ref.1, bf16[256,512]{1,0:T(8,128)(2,1)} %k_ref.1, bf16[256,512]{1,0:T(8,128)(2,1)} %v_ref.1, s32[2,128]{1,0:T(2,128)} %bitcast.1), custom_call_target="tpu_custom_call" | custom-call | tf_op jit(solution)/shard_map/attention/pallas_call | solution.py:411
  83.5 1.0 %copy.6 = bf16[128,4096]{1,0:T(8,128)(2,1)} copy(bf16[128,4096]{1,0:T(8,128)(2,1)S(1)} %attention.1) | data formatting | bytes 2097152

commit v5 on v4

--- a/solution.py
+++ b/solution.py
@@ -77,25 +77,29 @@
     mine = (BACK + y) * NZ + z
     pltpu.make_async_copy(k_ref.at[:, head_cols(y)], kv.at[mine, pl.ds(0, TOK)], y_recv.at[y]).start()
     pltpu.make_async_copy(seg_buf, kv.at[mine, pl.ds(2 * TOK, 16)], y_recv.at[y]).start()
+    pl.semaphore_wait(barrier, len(friends) + jnp.where(x > 0, 1, 0))
+
+    @pl.when(x > 0)
+    def _():
+        pl.semaphore_signal(ready, inc=1, device_id=dev(x_prev, y, z), device_id_type=pl.DeviceIdType.MESH)
+
+    sent = []
+
+    def to_peers(i, src_of, lo, rows):
+        for n, p in enumerate(y_peers):
+            copy = remote(src_of(p), kv.at[mine, pl.ds(lo, rows)], y_send.at[n, i], y_recv.at[y], dev(x, p, z))
+            copy.start()
+            sent.append(copy)
+
+    to_peers(0, lambda p: k_ref.at[:, head_cols(p)], 0, TOK)
+    to_peers(2, lambda p: seg_buf, 2 * TOK, 16)
     load_v.wait()
     for p in range(NY):
         turned = v_buf[:, p * DIM:(p + 1) * DIM].T
         vt_buf[p, :DIM, :] = turned[:, :DIM]
         vt_buf[p, DIM:, :] = turned[:, DIM:]
     pltpu.make_async_copy(vt_buf.at[y], kv.at[mine, pl.ds(TOK, TOK)], y_recv.at[y]).start()
-    pl.semaphore_wait(barrier, len(friends) + jnp.where(x > 0, 1, 0))
-
-    @pl.when(x > 0)
-    def _():
-        pl.semaphore_signal(ready, inc=1, device_id=dev(x_prev, y, z), device_id_type=pl.DeviceIdType.MESH)
-
-    sent = []
-    for n, p in enumerate(y_peers):
-        for i, (src, lo, rows) in enumerate(((k_ref.at[:, head_cols(p)], 0, TOK), (vt_buf.at[p], TOK, TOK),
-                                             (seg_buf, 2 * TOK, 16))):
-            copy = remote(src, kv.at[mine, pl.ds(lo, rows)], y_send.at[n, i], y_recv.at[y], dev(x, p, z))
-            copy.start()
-            sent.append(copy)
+    to_peers(1, lambda p: vt_buf.at[p], TOK, TOK)
 
     def shift_of(way, step):
         return step * (2 * way - 1)
@@ -294,22 +298,28 @@
             jobs.append((b, keys, turned_values(slots), None, True))
         chains(jobs)
 
+    def wait_for_x(step):
+        for way in range(2):
+            for row in (NY - 1, NY - 2):
+                wait_x(row, way, step)
+
+            @pl.when((step == 1) & side_comes(way))
+            def _():
+                side_copy(way).wait_recv()
+
     def later_step(step, _):
         def catch_up(j, _):
             @pl.when(step < half - 1)
             def _():
                 arrive(j, step + 1)
 
-            @pl.when(j == 2)
+            @pl.when((step > 1) & (j == 2))
             def _():
-                for way in range(2):
-                    for row in (NY - 1, NY - 2):
-                        wait_x(row, way, step)
-
-                    @pl.when((step == 1) & side_comes(way))
-                    def _():
-                        side_copy(way).wait_recv()
-            pair_work(1 - j // 2, j % 2, step)
+                wait_for_x(step - 1)
+
+            @pl.when((step > 1) | (j < 2))
+            def _():
+                pair_work(1 - j // 2, j % 2, step - j // 2)
             return 0
 
         lax.fori_loop(0, 4, catch_up, 0)
@@ -356,14 +366,23 @@
     def finish(j, _):
         @pl.when(j == 1)
         def _():
+            wait_for_x(half - 1)
+
+        @pl.when(j == 3)
+        def _():
             for row in (NY - 1, NY - 2):
                 wait_x(row, last_way(row), half)
-        pair_work(1 - j, 0, half)
-        for i in (1, 0):
-            send_back(2 * (1 - j) + i)
-        return 0
-
-    lax.fori_loop(0, 2, finish, 0)
+        last = (j == 0) | (j == 3)
+        pair = jnp.where(j == 0, 1, 0)
+        pair_work(pair, jnp.where(j == 2, 1, 0), jnp.where(last, half, half - 1))
+
+        @pl.when(last)
+        def _():
+            for i in (1, 0):
+                send_back(2 * pair + i)
+        return 0
+
+    lax.fori_loop(0, 4, finish, 0)
 
     for copy in sent + asked:
         copy.wait_send()

time: 84.7 us -> 85.4 us (level)
  no operation moved by 1% of the time
where the time goes in v5:
time: 85.4 us; the launch traced here: 85.1 us
  Pallas kernels  84.1 us (98%)
  local copies, waits for them, and re-layouts  0.97 us (1%)
    pallas_call x1, Pallas kernels, per_device(): pl.pallas_call(attention_kernel, out_shape=jax.ShapeDtypeStruct((TOK // 2...  84.1 us

profile of v5, /device:TPU:6, one launch (start us, length us, event | category | flops | bytes accessed | tf_op | source)
XLA Modules:
  0.0 85.1 jit_solution(13915544973835395519)
XLA Ops:
  0.0 84.1 %attention.1 = bf16[128,4096]{1,0:T(8,128)(2,1)S(1)} custom-call(bf16[256,2048]{1,0:T(8,128)(2,1)} %q_ref.1, bf16[256,512]{1,0:T(8,128)(2,1)} %k_ref.1, bf16[256,512]{1,0:T(8,128)(2,1)} %v_ref.1, s32[2,128]{1,0:T(2,128)} %bitcast.1), custom_call_target="tpu_custom_call" | custom-call | tf_op jit(solution)/shard_map/attention/pallas_call | solution.py:430
  84.1 1.0 %copy.6 = bf16[128,4096]{1,0:T(8,128)(2,1)} copy(bf16[128,4096]{1,0:T(8,128)(2,1)S(1)} %attention.1) | data formatting | bytes 2097152

commit v6 on v5

--- a/solution.py
+++ b/solution.py
@@ -14,6 +14,7 @@
 SLOTS = ROWS * NZ
 SLOT_ROWS = 2 * TOK + 16
 LANES = GROUP * TOK
+WIDE = 2 * TOK
 NEG = -1e30
 FAR_ID = 512.0
 SCALE = 1.4426950408889634 * DIM ** -0.5
@@ -235,35 +236,28 @@
         return jnp.concatenate([vt, jnp.ones((16, vt.shape[1]), jnp.bfloat16)], axis=0)
 
     def chains(jobs):
-        todo = [(b, slice(g * TOK, (g + 1) * TOK), keys, vt, bias, going)
-                for b, keys, vt, bias, going in jobs for g in range(GROUP)]
-        count = len(todo)
-        scores, weights, done = [None] * count, [None] * count, []
-        for i in range(count + 2):
-            if i < count:
-                b, cols, keys, _, _, _ = todo[i]
-                scores[i] = jnp.dot(keys, qe[b, :, cols], preferred_element_type=jnp.float32)
-            if 0 <= i - 1 < count:
-                b, cols, _, _, bias, going = todo[i - 1]
-                s = scores[i - 1]
-                if bias is not None:
-                    s = jnp.concatenate([s[:TOK] + bias, s[TOK:]], axis=0)
-                new = jnp.max(s, axis=0, keepdims=True)
-                fade = None
-                if going:
-                    old = peak[b, 0:1, cols]
-                    new = jnp.maximum(old, new)
-                    fade = jnp.exp2((old - new) * SCALE)
-                weights[i - 1] = (jnp.exp2((s - new) * SCALE).astype(jnp.bfloat16), new, fade)
-                scores[i - 1] = None
-            if i >= 2:
-                b, cols, _, vt, _, going = todo[i - 2]
-                w, new, fade = weights[i - 2]
-                done.append((b, cols, new, fade, jnp.dot(vt, w, preferred_element_type=jnp.float32)))
-                weights[i - 2] = None
-        for b, cols, new, fade, o in done:
+        todo = [(b, slice(g * WIDE, (g + 1) * WIDE), keys, vt, bias, going)
+                for b, keys, vt, bias, going in jobs for g in range(LANES // WIDE)]
+
+        def scores_of(b, cols, keys, vt, bias, going):
+            return jnp.dot(keys, qe[b, :, cols], preferred_element_type=jnp.float32)
+
+        ahead = scores_of(*todo[0])
+        for i, (b, cols, keys, vt, bias, going) in enumerate(todo):
+            s = ahead
+            if i + 1 < len(todo):
+                ahead = scores_of(*todo[i + 1])
+            if bias is not None:
+                s = jnp.concatenate([s[:TOK] + bias, s[TOK:]], axis=0)
+            new = jnp.max(s, axis=0, keepdims=True)
+            if going:
+                old = peak[b, 0:1, cols]
+                new = jnp.maximum(old, new)
+                fade = jnp.exp2((old - new) * SCALE)
+            w = jnp.exp2(s * SCALE - new * SCALE).astype(jnp.bfloat16)
+            o = jnp.dot(vt, w, preferred_element_type=jnp.float32)
             peak[b, 0:1, cols] = new
-            acc[b, :, cols] = o if fade is None else acc[b, :, cols] * fade + o
+            acc[b, :, cols] = acc[b, :, cols] * fade + o if going else o
 
     def own_work(j, _):
         jobs = []
@@ -278,7 +272,7 @@
             rest = jnp.concatenate([jnp.where(row == begin, 0.0, NEG)] * GROUP, axis=1)
             which = lax.broadcasted_iota(jnp.int32, (DIM, LANES), 0)
             qe[b, DIM:, :] = jnp.where(which == 0, 1.0, jnp.where(which == 1, rest, 0.0)).astype(jnp.bfloat16)
-            bias = jnp.where((rows == rows.T) & (key <= token), 0.0, NEG)
+            bias = jnp.concatenate([jnp.where((rows == rows.T) & (key <= token), 0.0, NEG)] * (WIDE // TOK), axis=1)
             early = [slot(b - 1, 0), slot(b - 2, 0)]
             keys = jnp.concatenate([own_keys(at)] + [early_keys(one, b) for one in early], axis=0)
             jobs.append((b, keys, turned_values([at] + early), bias, False))
@@ -287,13 +281,15 @@
 
     lax.fori_loop(0, NY // 2, own_work, 0)
 
-    def pair_work(pair, way, step):
-        shift = shift_of(way, step)
-        there = lax.rem(z + shift + NZ, NZ)
+    def pair_work(pair, ways, step):
         jobs = []
         for i in (1, 0):
             b = 2 * pair + i
-            slots = [slot(b - 1, shift), slot(jnp.where(there < z, b, b - 2), shift)]
+            slots = []
+            for way in ways:
+                shift = shift_of(way, step)
+                there = lax.rem(z + shift + NZ, NZ)
+                slots += [slot(b - 1, shift), slot(jnp.where(there < z, b, b - 2), shift)]
             keys = jnp.concatenate([early_keys(at, b) for at in slots], axis=0)
             jobs.append((b, keys, turned_values(slots), None, True))
         chains(jobs)
@@ -311,18 +307,19 @@
         def catch_up(j, _):
             @pl.when(step < half - 1)
             def _():
-                arrive(j, step + 1)
-
-            @pl.when((step > 1) & (j == 2))
+                arrive(2 * j, step + 1)
+                arrive(2 * j + 1, step + 1)
+
+            @pl.when((step > 1) & (j == 1))
             def _():
                 wait_for_x(step - 1)
 
-            @pl.when((step > 1) | (j < 2))
+            @pl.when((step > 1) | (j == 0))
             def _():
-                pair_work(1 - j // 2, j % 2, step - j // 2)
+                pair_work(1 - j, (0, 1), step - j)
             return 0
 
-        lax.fori_loop(0, 4, catch_up, 0)
+        lax.fori_loop(0, 2, catch_up, 0)
         return 0
 
     lax.fori_loop(1, half, later_step, 0)
@@ -367,22 +364,15 @@
         @pl.when(j == 1)
         def _():
             wait_for_x(half - 1)
-
-        @pl.when(j == 3)
-        def _():
+            pair_work(0, (0, 1), half - 1)
             for row in (NY - 1, NY - 2):
                 wait_x(row, last_way(row), half)
-        last = (j == 0) | (j == 3)
-        pair = jnp.where(j == 0, 1, 0)
-        pair_work(pair, jnp.where(j == 2, 1, 0), jnp.where(last, half, half - 1))
-
-        @pl.when(last)
-        def _():
-            for i in (1, 0):
-                send_back(2 * pair + i)
-        return 0
-
-    lax.fori_loop(0, 4, finish, 0)
+        pair_work(1 - j, (0,), half)
+        for i in (1, 0):
+            send_back(2 * (1 - j) + i)
+        return 0
+
+    lax.fori_loop(0, 2, finish, 0)
 
     for copy in sent + asked:
         copy.wait_send()

time: 85.4 us -> 85.3 us (level)
  no operation moved by 1% of the time
where the time goes in v6:
time: 85.3 us; the launch traced here: 85 us
  Pallas kernels  84 us (98%)
  local copies, waits for them, and re-layouts  0.97 us (1%)
    pallas_call x1, Pallas kernels, per_device(): pl.pallas_call(attention_kernel, out_shape=jax.ShapeDtypeStruct((TOK // 2...  84 us

profile of v6, /device:TPU:6, one launch (start us, length us, event | category | flops | bytes accessed | tf_op | source)
XLA Modules:
  0.0 85.0 jit_solution(2669569700606197400)
XLA Ops:
  0.0 84.0 %attention.1 = bf16[128,4096]{1,0:T(8,128)(2,1)S(1)} custom-call(bf16[256,2048]{1,0:T(8,128)(2,1)} %q_ref.1, bf16[256,512]{1,0:T(8,128)(2,1)} %k_ref.1, bf16[256,512]{1,0:T(8,128)(2,1)} %v_ref.1, s32[2,128]{1,0:T(2,128)} %bitcast.1), custom_call_target="tpu_custom_call" | custom-call | tf_op jit(solution)/shard_map/attention/pallas_call | solution.py:420
  84.0 1.0 %copy.6 = bf16[128,4096]{1,0:T(8,128)(2,1)} copy(bf16[128,4096]{1,0:T(8,128)(2,1)S(1)} %attention.1) | data formatting | bytes 2097152

commit v7 on v6

--- a/solution.py
+++ b/solution.py
@@ -37,7 +37,8 @@
 def attention_kernel(q_ref, k_ref, v_ref, seg_ref, out_ref, q_buf, v_buf, seg_in, seg_buf, vt_buf, qt_buf,
                      kv, qe, acc, peak, first, o_buf, load_sem,
                      y_send, y_recv, q_send, q_recv, z_send, z_recv, x_send, x_recv,
-                     side_send, side_recv, ready, o_send, o_recv):
+                     side_send, side_recv, ready, o_send, o_recv,
+                     k_box, v_box, q_box, o_box, r_send, r_recv, f_send):
     me, x, y, z = place()
     core = lax.axis_index("kvh")
     half = NZ // 2
@@ -84,23 +85,35 @@
     def _():
         pl.semaphore_signal(ready, inc=1, device_id=dev(x_prev, y, z), device_id_type=pl.DeviceIdType.MESH)
 
+    up, across, down = y_peers
     sent = []
 
-    def to_peers(i, src_of, lo, rows):
-        for n, p in enumerate(y_peers):
-            copy = remote(src_of(p), kv.at[mine, pl.ds(lo, rows)], y_send.at[n, i], y_recv.at[y], dev(x, p, z))
-            copy.start()
-            sent.append(copy)
-
-    to_peers(0, lambda p: k_ref.at[:, head_cols(p)], 0, TOK)
-    to_peers(2, lambda p: seg_buf, 2 * TOK, 16)
+    def through(part, src, box):
+        return remote(src, box, r_send.at[part], r_recv.at[part], dev(x, down if part % 2 else up, z))
+
+    def direct(i, src, lo, rows, n):
+        copy = remote(src, kv.at[mine, pl.ds(lo, rows)], y_send.at[n, i], y_recv.at[y], dev(x, y_peers[n], z))
+        copy.start()
+        sent.append(copy)
+
+    def send(copy):
+        copy.start()
+        sent.append(copy)
+
+    send(through(0, k_ref.at[:, head_cols(across)], k_box))
+    for n in (0, 2):
+        direct(0, k_ref.at[:, head_cols(y_peers[n])], 0, TOK, n)
     load_v.wait()
     for p in range(NY):
         turned = v_buf[:, p * DIM:(p + 1) * DIM].T
         vt_buf[p, :DIM, :] = turned[:, :DIM]
         vt_buf[p, DIM:, :] = turned[:, DIM:]
     pltpu.make_async_copy(vt_buf.at[y], kv.at[mine, pl.ds(TOK, TOK)], y_recv.at[y]).start()
-    to_peers(1, lambda p: vt_buf.at[p], TOK, TOK)
+    send(through(1, vt_buf.at[across], v_box))
+    for n in (0, 2):
+        direct(1, vt_buf.at[y_peers[n]], TOK, TOK, n)
+    for n in range(NY - 1):
+        direct(2, seg_buf, 2 * TOK, 16, n)
 
     def shift_of(way, step):
         return step * (2 * way - 1)
@@ -156,21 +169,33 @@
         z_copy(1, row, 1).start()
         return 0
 
-    lax.fori_loop(0, NY, first_sends, 0)
+    lax.fori_loop(0, 1, first_sends, 0)
+    load_q.wait()
+    for p in range(NY):
+        for g in range(GROUP):
+            h = p * GROUP + g
+            qt_buf[p, :, g * TOK:(g + 1) * TOK] = q_buf[:, h * DIM:(h + 1) * DIM].T
+
+    def pass_through(part, box, dst, recv, device):
+        pltpu.make_async_copy(box, box, r_recv.at[part]).wait()
+        send(remote(box, dst, f_send.at[part], recv, device))
+
+    up_dev, down_dev = dev(x, up, z), dev(x, down, z)
+    pass_through(0, k_box, kv.at[slot(down, 0), pl.ds(0, TOK)], y_recv.at[down], up_dev)
+    pass_through(1, v_box, kv.at[slot(up, 0), pl.ds(TOK, TOK)], y_recv.at[up], down_dev)
+    lax.fori_loop(1, NY, first_sends, 0)
 
     @pl.when(x < NX - 1)
     def _():
         pl.semaphore_wait(ready, 1)
     forward(0, NY - 1, 0)
     forward(0, NY - 2, 0)
-    load_q.wait()
-    for p in range(NY):
-        for g in range(GROUP):
-            h = p * GROUP + g
-            qt_buf[p, :, g * TOK:(g + 1) * TOK] = q_buf[:, h * DIM:(h + 1) * DIM].T
+    part_rows = DIM // 2
+    send(through(2, qt_buf.at[across, pl.ds(0, part_rows)], q_box.at[0]))
+    send(through(3, qt_buf.at[across, pl.ds(part_rows, part_rows)], q_box.at[1]))
     asked = []
-    for n, p in enumerate(y_peers):
-        copy = remote(qt_buf.at[p], qe.at[y, pl.ds(0, DIM)], q_send.at[n], q_recv.at[n], dev(x, p, z))
+    for n in (0, 2):
+        copy = remote(qt_buf.at[y_peers[n]], qe.at[y, pl.ds(0, DIM)], q_send.at[n], q_recv.at[n], dev(x, y_peers[n], z))
         copy.start()
         asked.append(copy)
     own_q = pltpu.make_async_copy(qt_buf.at[y], qe.at[y, pl.ds(0, DIM)], q_send.at[NY - 1])
@@ -197,7 +222,10 @@
         arrive(i, 1)
         return 0
 
-    lax.fori_loop(0, NY, first_step, 0)
+    lax.fori_loop(0, 2, first_step, 0)
+    pass_through(2, q_box.at[0], qe.at[down, pl.ds(0, part_rows)], q_recv.at[1], up_dev)
+    pass_through(3, q_box.at[1], qe.at[up, pl.ds(part_rows, part_rows)], q_recv.at[1], down_dev)
+    lax.fori_loop(2, NY, first_step, 0)
 
     def wait_x(row, way, step):
         @pl.when(over_x(way, row, step) & (x > 0))
@@ -212,6 +240,8 @@
             side_copy(way).start()
     for copy in asked:
         copy.wait_recv()
+    far_q = qe.at[across, pl.ds(0, DIM)]
+    pltpu.make_async_copy(far_q, far_q, q_recv.at[1]).wait()
     own_q.wait()
 
     key = lax.broadcasted_iota(jnp.int32, (TOK, TOK), 0)
@@ -277,6 +307,8 @@
             keys = jnp.concatenate([own_keys(at)] + [early_keys(one, b) for one in early], axis=0)
             jobs.append((b, keys, turned_values([at] + early), bias, False))
         chains(jobs)
+        arrive(2 * j, 2)
+        arrive(2 * j + 1, 2)
         return 0
 
     lax.fori_loop(0, NY // 2, own_work, 0)
@@ -305,30 +337,21 @@
 
     def later_step(step, _):
         def catch_up(j, _):
+            @pl.when(j == 1)
+            def _():
+                wait_for_x(step)
+            pair_work(1 - j, (0, 1), step)
+
             @pl.when(step < half - 1)
             def _():
-                arrive(2 * j, step + 1)
-                arrive(2 * j + 1, step + 1)
-
-            @pl.when((step > 1) & (j == 1))
-            def _():
-                wait_for_x(step - 1)
-
-            @pl.when((step > 1) | (j == 0))
-            def _():
-                pair_work(1 - j, (0, 1), step - j)
+                arrive(2 * j, step + 2)
+                arrive(2 * j + 1, step + 2)
             return 0
 
-        lax.fori_loop(0, 2, catch_up, 0)
+        lax.fori_loop(0, 2 - step // (half - 1), catch_up, 0)
         return 0
 
     lax.fori_loop(1, half, later_step, 0)
-
-    def last_step(i, _):
-        arrive(i, half)
-        return 0
-
-    lax.fori_loop(0, NY, last_step, 0)
 
     rows = TOK // 2
     wide = GROUP * DIM
@@ -350,21 +373,51 @@
         mixed = (acc[b, :DIM, :] * (1.0 / acc[b, DIM:DIM + 1, :])).astype(jnp.bfloat16)
         for g in range(GROUP):
             o_buf[b, :, g * DIM:(g + 1) * DIM] = mixed[:, g * TOK:(g + 1) * TOK].T
-        over(b).start()
-
-        @pl.when(b != y)
+
+        @pl.when(b == across)
+        def _():
+            through(4, part(b, core), o_box.at[0]).start()
+            through(5, part(b, 1 - core), o_box.at[1]).start()
+
+        @pl.when(b != across)
+        def _():
+            over(b).start()
+
+        @pl.when((b != across) & (b != y))
         def _():
             along(b).start()
 
         @pl.when(b == y)
         def _():
             stay(b).start()
+
+    def cols_of(source):
+        return out_ref.at[:, pl.ds(pl.multiple_of((core * NY + source) * wide, wide), wide)]
+
+    def output_through(part):
+        pltpu.make_async_copy(o_box.at[part - 4], o_box.at[part - 4], r_recv.at[part]).wait()
+        output_on(part).start()
+
+    def output_on(part):
+        if part == 4:
+            return remote(o_box.at[0], cols_of(down), f_send.at[4], o_recv.at[down, 0], up_dev)
+        return remote(o_box.at[1], cols_of(up), f_send.at[5], o_recv.at[up, 1], (index_of(x, down, z), 1 - core))
+
+    early = (y == 1) | (y == 2)
 
     def finish(j, _):
         @pl.when(j == 1)
         def _():
             wait_for_x(half - 1)
             pair_work(0, (0, 1), half - 1)
+
+            @pl.when(early)
+            def _():
+                output_through(4)
+
+            @pl.when(jnp.logical_not(early))
+            def _():
+                output_through(5)
             for row in (NY - 1, NY - 2):
                 wait_x(row, last_way(row), half)
         pair_work(1 - j, (0,), half)
@@ -374,6 +427,14 @@
 
     lax.fori_loop(0, 2, finish, 0)
 
+    @pl.when(early)
+    def _():
+        output_through(5)
+
+    @pl.when(jnp.logical_not(early))
+    def _():
+        output_through(4)
+
     for copy in sent + asked:
         copy.wait_send()
 
@@ -401,10 +462,16 @@
         @pl.when(side_goes(way))
         def _():
             side_copy(way).wait_send()
+    through(4, part(across, core), o_box.at[0]).wait_send()
+    through(5, part(across, 1 - core), o_box.at[1]).wait_send()
+    output_on(4).wait_send()
+    output_on(5).wait_send()
     for b in range(NY):
-        over(b).wait_send()
-
-        @pl.when(b != y)
+        @pl.when(b != across)
+        def _():
+            over(b).wait_send()
+
+        @pl.when((b != y) & (b != across))
         def _():
             along(b).wait_send()
         for e in range(2):
@@ -430,7 +497,9 @@
             pltpu.VMEM((NY, 8, 128), f32), pltpu.VMEM((NY, TOK, GROUP * DIM), bf16),
             dma((3,)), dma((NY - 1, 3)), dma((NY,)), dma((NY,)), dma((NY - 1,)),
             dma((2, NY, half)), dma((2, NY, half)), dma((BACK, 2, half + 1)), dma((BACK, 2, half + 1)),
-            dma((2,)), dma((2,)), pltpu.SemaphoreType.REGULAR, dma((NY, 2)), dma((NY, 2))],
+            dma((2,)), dma((2,)), pltpu.SemaphoreType.REGULAR, dma((NY, 2)), dma((NY, 2)),
+            pltpu.VMEM((TOK, DIM), bf16), pltpu.VMEM((TOK, DIM), bf16), pltpu.VMEM((2, DIM // 2, LANES), bf16),
+            pltpu.VMEM((2, TOK // 2, GROUP * DIM), bf16), dma((6,)), dma((6,)), dma((6,))],
         compiler_params=pltpu.CompilerParams(collective_id=0, has_side_effects=True,
                                              vmem_limit_bytes=40 * 1024 * 1024),
         name="attention",

time: 85.3 us -> 86.9 us (1.019)
  Pallas kernels: 84 us -> 85.8 us
    pallas_call x1, Pallas kernels: 84 us -> 85.8 us  [per_device(): pl.pallas_call(attention_kernel, out_shape=jax.ShapeDtypeStruct((TOK // 2...]
where the time goes in v7:
time: 86.9 us; the launch traced here: 86.8 us
  Pallas kernels  85.8 us (99%)
  local copies, waits for them, and re-layouts  0.97 us (1%)
    pallas_call x1, Pallas kernels, per_device(): pl.pallas_call(attention_kernel, out_shape=jax.ShapeDtypeStruct((TOK // 2...  85.8 us

profile of v7, /device:TPU:6, one launch (start us, length us, event | category | flops | bytes accessed | tf_op | source)
XLA Modules:
  0.0 86.8 jit_solution(4904151413755094649)
XLA Ops:
  0.0 85.8 %attention.1 = bf16[128,4096]{1,0:T(8,128)(2,1)S(1)} custom-call(bf16[256,2048]{1,0:T(8,128)(2,1)} %q_ref.1, bf16[256,512]{1,0:T(8,128)(2,1)} %k_ref.1, bf16[256,512]{1,0:T(8,128)(2,1)} %v_ref.1, s32[2,128]{1,0:T(2,128)} %bitcast.1), custom_call_target="tpu_custom_call" | custom-call | tf_op jit(solution)/shard_map/attention/pallas_call | solution.py:487
  85.8 1.0 %copy.6 = bf16[128,4096]{1,0:T(8,128)(2,1)} copy(bf16[128,4096]{1,0:T(8,128)(2,1)S(1)} %attention.1) | data formatting | bytes 2097152

commit v8 on v7

--- a/solution.py
+++ b/solution.py
@@ -14,7 +14,8 @@
 SLOTS = ROWS * NZ
 SLOT_ROWS = 2 * TOK + 16
 LANES = GROUP * TOK
-WIDE = 2 * TOK
+WIDE = TOK
+PIECES = 2
 NEG = -1e30
 FAR_ID = 512.0
 SCALE = 1.4426950408889634 * DIM ** -0.5
@@ -268,26 +269,54 @@
     def chains(jobs):
         todo = [(b, slice(g * WIDE, (g + 1) * WIDE), keys, vt, bias, going)
                 for b, keys, vt, bias, going in jobs for g in range(LANES // WIDE)]
-
-        def scores_of(b, cols, keys, vt, bias, going):
-            return jnp.dot(keys, qe[b, :, cols], preferred_element_type=jnp.float32)
-
-        ahead = scores_of(*todo[0])
+        count = len(todo)
+
+        def scores_of(i, n):
+            b, cols, keys, _, bias, _ = todo[i]
+            size = keys.shape[0] // PIECES
+            s = jnp.dot(keys[n * size:(n + 1) * size], qe[b, :, cols], preferred_element_type=jnp.float32)
+            if bias is not None and n == 0:
+                s = jnp.concatenate([s[:TOK] + bias, s[TOK:]], axis=0)
+            return s, jnp.max(s, axis=0, keepdims=True)
+
+        def weigh(i, n, s, shift):
+            return jnp.exp2(s * SCALE - shift).astype(jnp.bfloat16)
+
+        def values_of(i, n, w, o):
+            vt = todo[i][3]
+            size = vt.shape[1] // PIECES
+            more = jnp.dot(vt[:, n * size:(n + 1) * size], w, preferred_element_type=jnp.float32)
+            return more if o is None else o + more
+
+        ahead = [scores_of(0, n) for n in range(PIECES)]
+        late = None
         for i, (b, cols, keys, vt, bias, going) in enumerate(todo):
-            s = ahead
-            if i + 1 < len(todo):
-                ahead = scores_of(*todo[i + 1])
-            if bias is not None:
-                s = jnp.concatenate([s[:TOK] + bias, s[TOK:]], axis=0)
-            new = jnp.max(s, axis=0, keepdims=True)
+            held, ahead = ahead, []
+            new = held[0][1]
+            for _, top in held[1:]:
+                new = jnp.maximum(new, top)
+            fade = None
             if going:
                 old = peak[b, 0:1, cols]
                 new = jnp.maximum(old, new)
                 fade = jnp.exp2((old - new) * SCALE)
-            w = jnp.exp2(s * SCALE - new * SCALE).astype(jnp.bfloat16)
-            o = jnp.dot(vt, w, preferred_element_type=jnp.float32)
             peak[b, 0:1, cols] = new
-            acc[b, :, cols] = acc[b, :, cols] * fade + o if going else o
+            shift = new * SCALE
+            o = None
+            for n in range(PIECES):
+                if i + 1 < count:
+                    ahead.append(scores_of(i + 1, n))
+                w = weigh(i, n, held[n][0], shift)
+                if late is not None:
+                    late()
+                    late = None
+                if n + 1 < PIECES:
+                    o = values_of(i, n, w, o)
+
+            def late(i=i, w=w, o=o, b=b, cols=cols, fade=fade):
+                total = values_of(i, PIECES - 1, w, o)
+                acc[b, :, cols] = total if fade is None else acc[b, :, cols] * fade + total
+        late()
 
     def own_work(j, _):
         jobs = []

time: 86.9 us -> 85.9 us (0.988)
  Pallas kernels: 85.8 us -> 84.8 us
    pallas_call x1, Pallas kernels: 85.8 us -> 84.8 us  [per_device(): pl.pallas_call(attention_kernel, out_shape=jax.ShapeDtypeStruct((TOK // 2...]
where the time goes in v8:
time: 85.9 us; the launch traced here: 85.8 us
  Pallas kernels  84.8 us (99%)
  local copies, waits for them, and re-layouts  0.97 us (1%)
    pallas_call x1, Pallas kernels, per_device(): pl.pallas_call(attention_kernel, out_shape=jax.ShapeDtypeStruct((TOK // 2...  84.8 us

profile of v8, /device:TPU:6, one launch (start us, length us, event | category | flops | bytes accessed | tf_op | source)
XLA Modules:
  0.0 85.8 jit_solution(5547205923802626475)
XLA Ops:
  0.0 84.8 %attention.1 = bf16[128,4096]{1,0:T(8,128)(2,1)S(1)} custom-call(bf16[256,2048]{1,0:T(8,128)(2,1)} %q_ref.1, bf16[256,512]{1,0:T(8,128)(2,1)} %k_ref.1, bf16[256,512]{1,0:T(8,128)(2,1)} %v_ref.1, s32[2,128]{1,0:T(2,128)} %bitcast.1), custom_call_target="tpu_custom_call" | custom-call | tf_op jit(solution)/shard_map/attention/pallas_call | solution.py:516
  84.8 1.0 %copy.6 = bf16[128,4096]{1,0:T(8,128)(2,1)} copy(bf16[128,4096]{1,0:T(8,128)(2,1)S(1)} %attention.1) | data formatting | bytes 2097152

commit v9 on v8

--- a/solution.py
+++ b/solution.py
@@ -14,7 +14,7 @@
 SLOTS = ROWS * NZ
 SLOT_ROWS = 2 * TOK + 16
 LANES = GROUP * TOK
-WIDE = TOK
+WIDE = LANES
 PIECES = 2
 NEG = -1e30
 FAR_ID = 512.0
@@ -80,41 +80,40 @@
     mine = (BACK + y) * NZ + z
     pltpu.make_async_copy(k_ref.at[:, head_cols(y)], kv.at[mine, pl.ds(0, TOK)], y_recv.at[y]).start()
     pltpu.make_async_copy(seg_buf, kv.at[mine, pl.ds(2 * TOK, 16)], y_recv.at[y]).start()
-    pl.semaphore_wait(barrier, len(friends) + jnp.where(x > 0, 1, 0))
-
-    @pl.when(x > 0)
-    def _():
-        pl.semaphore_signal(ready, inc=1, device_id=dev(x_prev, y, z), device_id_type=pl.DeviceIdType.MESH)
-
-    up, across, down = y_peers
-    sent = []
-
-    def through(part, src, box):
-        return remote(src, box, r_send.at[part], r_recv.at[part], dev(x, down if part % 2 else up, z))
-
-    def direct(i, src, lo, rows, n):
-        copy = remote(src, kv.at[mine, pl.ds(lo, rows)], y_send.at[n, i], y_recv.at[y], dev(x, y_peers[n], z))
-        copy.start()
-        sent.append(copy)
-
-    def send(copy):
-        copy.start()
-        sent.append(copy)
-
-    send(through(0, k_ref.at[:, head_cols(across)], k_box))
-    for n in (0, 2):
-        direct(0, k_ref.at[:, head_cols(y_peers[n])], 0, TOK, n)
     load_v.wait()
     for p in range(NY):
         turned = v_buf[:, p * DIM:(p + 1) * DIM].T
         vt_buf[p, :DIM, :] = turned[:, :DIM]
         vt_buf[p, DIM:, :] = turned[:, DIM:]
     pltpu.make_async_copy(vt_buf.at[y], kv.at[mine, pl.ds(TOK, TOK)], y_recv.at[y]).start()
+    pl.semaphore_wait(barrier, len(friends) + jnp.where(x > 0, 1, 0))
+
+    @pl.when(x > 0)
+    def _():
+        pl.semaphore_signal(ready, inc=1, device_id=dev(x_prev, y, z), device_id_type=pl.DeviceIdType.MESH)
+
+    up, across, down = y_peers
+    sent = []
+
+    def through(part, src, box):
+        return remote(src, box, r_send.at[part], r_recv.at[part], dev(x, down if part % 2 else up, z))
+
+    def direct(i, src, lo, rows, n):
+        copy = remote(src, kv.at[mine, pl.ds(lo, rows)], y_send.at[n, i], y_recv.at[y], dev(x, y_peers[n], z))
+        copy.start()
+        sent.append(copy)
+
+    def send(copy):
+        copy.start()
+        sent.append(copy)
+
+    send(through(0, k_ref.at[:, head_cols(across)], k_box))
     send(through(1, vt_buf.at[across], v_box))
     for n in (0, 2):
+        direct(0, k_ref.at[:, head_cols(y_peers[n])], 0, TOK, n)
         direct(1, vt_buf.at[y_peers[n]], TOK, TOK, n)
-    for n in range(NY - 1):
         direct(2, seg_buf, 2 * TOK, 16, n)
+    direct(2, seg_buf, 2 * TOK, 16, 1)
 
     def shift_of(way, step):
         return step * (2 * way - 1)
@@ -171,26 +170,26 @@
         return 0
 
     lax.fori_loop(0, 1, first_sends, 0)
+
+    def pass_through(part, box, dst, recv, device):
+        pltpu.make_async_copy(box, box, r_recv.at[part]).wait()
+        send(remote(box, dst, f_send.at[part], recv, device))
+
+    up_dev, down_dev = dev(x, up, z), dev(x, down, z)
+    pass_through(0, k_box, kv.at[slot(down, 0), pl.ds(0, TOK)], y_recv.at[down], up_dev)
+    pass_through(1, v_box, kv.at[slot(up, 0), pl.ds(TOK, TOK)], y_recv.at[up], down_dev)
+    lax.fori_loop(1, NY, first_sends, 0)
+
+    @pl.when(x < NX - 1)
+    def _():
+        pl.semaphore_wait(ready, 1)
+    forward(0, NY - 1, 0)
+    forward(0, NY - 2, 0)
     load_q.wait()
     for p in range(NY):
         for g in range(GROUP):
             h = p * GROUP + g
             qt_buf[p, :, g * TOK:(g + 1) * TOK] = q_buf[:, h * DIM:(h + 1) * DIM].T
-
-    def pass_through(part, box, dst, recv, device):
-        pltpu.make_async_copy(box, box, r_recv.at[part]).wait()
-        send(remote(box, dst, f_send.at[part], recv, device))
-
-    up_dev, down_dev = dev(x, up, z), dev(x, down, z)
-    pass_through(0, k_box, kv.at[slot(down, 0), pl.ds(0, TOK)], y_recv.at[down], up_dev)
-    pass_through(1, v_box, kv.at[slot(up, 0), pl.ds(TOK, TOK)], y_recv.at[up], down_dev)
-    lax.fori_loop(1, NY, first_sends, 0)
-
-    @pl.when(x < NX - 1)
-    def _():
-        pl.semaphore_wait(ready, 1)
-    forward(0, NY - 1, 0)
-    forward(0, NY - 2, 0)
     part_rows = DIM // 2
     send(through(2, qt_buf.at[across, pl.ds(0, part_rows)], q_box.at[0]))
     send(through(3, qt_buf.at[across, pl.ds(part_rows, part_rows)], q_box.at[1]))

time: 85.9 us -> 85 us (0.990)
  Pallas kernels: 84.8 us -> 83.9 us
where the time goes in v9:
time: 85 us; the launch traced here: 84.9 us
  Pallas kernels  83.9 us (99%)
  local copies, waits for them, and re-layouts  0.97 us (1%)
    pallas_call x1, Pallas kernels, per_device(): pl.pallas_call(attention_kernel, out_shape=jax.ShapeDtypeStruct((TOK // 2...  83.9 us

profile of v9, /device:TPU:6, one launch (start us, length us, event | category | flops | bytes accessed | tf_op | source)
XLA Modules:
  0.0 84.9 jit_solution(14880124429480329880)
XLA Ops:
  0.0 83.9 %attention.1 = bf16[128,4096]{1,0:T(8,128)(2,1)S(1)} custom-call(bf16[256,2048]{1,0:T(8,128)(2,1)} %q_ref.1, bf16[256,512]{1,0:T(8,128)(2,1)} %k_ref.1, bf16[256,512]{1,0:T(8,128)(2,1)} %v_ref.1, s32[2,128]{1,0:T(2,128)} %bitcast.1), custom_call_target="tpu_custom_call" | custom-call | tf_op jit(solution)/shard_map/attention/pallas_call | solution.py:515
  83.9 1.0 %copy.6 = bf16[128,4096]{1,0:T(8,128)(2,1)} copy(bf16[128,4096]{1,0:T(8,128)(2,1)S(1)} %attention.1) | data formatting | bytes 2097152

commit v10 on v9

--- a/solution.py
+++ b/solution.py
@@ -19,6 +19,7 @@
 NEG = -1e30
 FAR_ID = 512.0
 SCALE = 1.4426950408889634 * DIM ** -0.5
+LN2 = 0.6931471805599453
 
 
 def place():
@@ -279,7 +280,11 @@
             return s, jnp.max(s, axis=0, keepdims=True)
 
         def weigh(i, n, s, shift):
-            return jnp.exp2(s * SCALE - shift).astype(jnp.bfloat16)
+            power = s * SCALE - shift
+            high = power.astype(jnp.bfloat16)
+            low = ((power - high.astype(jnp.float32)) * LN2).astype(jnp.bfloat16)
+            w = jnp.exp2(high)
+            return w + w * low
 
         def values_of(i, n, w, o):
             vt = todo[i][3]

time: 85 us -> 93.2 us (1.096)
  Pallas kernels: 83.9 us -> 92.1 us
    pallas_call x1, Pallas kernels: 83.9 us -> 92.1 us  [per_device(): pl.pallas_call(attention_kernel, out_shape=jax.ShapeDtypeStruct((TOK // 2...]
where the time goes in v10:
time: 93.2 us; the launch traced here: 93.1 us
  Pallas kernels  92.1 us (99%)
  local copies, waits for them, and re-layouts  0.97 us (1%)
    pallas_call x1, Pallas kernels, per_device(): pl.pallas_call(attention_kernel, out_shape=jax.ShapeDtypeStruct((TOK // 2...  92.1 us

profile of v10, /device:TPU:6, one launch (start us, length us, event | category | flops | bytes accessed | tf_op | source)
XLA Modules:
  0.0 93.1 jit_solution(8868606204387773937)
XLA Ops:
  0.0 92.1 %attention.1 = bf16[128,4096]{1,0:T(8,128)(2,1)S(1)} custom-call(bf16[256,2048]{1,0:T(8,128)(2,1)} %q_ref.1, bf16[256,512]{1,0:T(8,128)(2,1)} %k_ref.1, bf16[256,512]{1,0:T(8,128)(2,1)} %v_ref.1, s32[2,128]{1,0:T(2,128)} %bitcast.1), custom_call_target="tpu_custom_call" | custom-call | tf_op jit(solution)/shard_map/attention/pallas_call | solution.py:520
  92.1 1.0 %copy.6 = bf16[128,4096]{1,0:T(8,128)(2,1)} copy(bf16[128,4096]{1,0:T(8,128)(2,1)S(1)} %attention.1) | data formatting | bytes 2097152

commit v11 on v9

--- a/solution.py
+++ b/solution.py
@@ -14,7 +14,7 @@
 SLOTS = ROWS * NZ
 SLOT_ROWS = 2 * TOK + 16
 LANES = GROUP * TOK
-WIDE = LANES
+WIDE = TOK
 PIECES = 2
 NEG = -1e30
 FAR_ID = 512.0
@@ -238,6 +238,8 @@
         @pl.when(side_goes(way))
         def _():
             side_copy(way).start()
+    arrive(0, 2)
+    arrive(1, 2)
     for copy in asked:
         copy.wait_recv()
     far_q = qe.at[across, pl.ds(0, DIM)]
@@ -318,41 +320,36 @@
         late()
 
     def own_work(j, _):
-        jobs = []
-        for i in (1, 0):
-            b = NY - 2 - 2 * j + i
-            at = slot(b, 0)
-            own = kv[at, 2 * TOK:, :].astype(jnp.float32)
-            row = jnp.concatenate([own[0:1], own[1:2]], axis=1)
-            rows = jnp.broadcast_to(row, (TOK, TOK))
-            begin = row[:, 0:1]
-            first[b] = jnp.broadcast_to(begin, (8, 128))
-            rest = jnp.concatenate([jnp.where(row == begin, 0.0, NEG)] * GROUP, axis=1)
-            which = lax.broadcasted_iota(jnp.int32, (DIM, LANES), 0)
-            qe[b, DIM:, :] = jnp.where(which == 0, 1.0, jnp.where(which == 1, rest, 0.0)).astype(jnp.bfloat16)
-            bias = jnp.concatenate([jnp.where((rows == rows.T) & (key <= token), 0.0, NEG)] * (WIDE // TOK), axis=1)
-            early = [slot(b - 1, 0), slot(b - 2, 0)]
-            keys = jnp.concatenate([own_keys(at)] + [early_keys(one, b) for one in early], axis=0)
-            jobs.append((b, keys, turned_values([at] + early), bias, False))
-        chains(jobs)
-        arrive(2 * j, 2)
-        arrive(2 * j + 1, 2)
-        return 0
-
-    lax.fori_loop(0, NY // 2, own_work, 0)
-
-    def pair_work(pair, ways, step):
-        jobs = []
-        for i in (1, 0):
-            b = 2 * pair + i
-            slots = []
-            for way in ways:
-                shift = shift_of(way, step)
-                there = lax.rem(z + shift + NZ, NZ)
-                slots += [slot(b - 1, shift), slot(jnp.where(there < z, b, b - 2), shift)]
-            keys = jnp.concatenate([early_keys(at, b) for at in slots], axis=0)
-            jobs.append((b, keys, turned_values(slots), None, True))
-        chains(jobs)
+        b = NY - 1 - j
+        at = slot(b, 0)
+        own = kv[at, 2 * TOK:, :].astype(jnp.float32)
+        row = jnp.concatenate([own[0:1], own[1:2]], axis=1)
+        rows = jnp.broadcast_to(row, (TOK, TOK))
+        begin = row[:, 0:1]
+        first[b] = jnp.broadcast_to(begin, (8, 128))
+        rest = jnp.concatenate([jnp.where(row == begin, 0.0, NEG)] * GROUP, axis=1)
+        which = lax.broadcasted_iota(jnp.int32, (DIM, LANES), 0)
+        qe[b, DIM:, :] = jnp.where(which == 0, 1.0, jnp.where(which == 1, rest, 0.0)).astype(jnp.bfloat16)
+        bias = jnp.concatenate([jnp.where((rows == rows.T) & (key <= token), 0.0, NEG)] * (WIDE // TOK), axis=1)
+        early = [slot(b - 1, 0), slot(b - 2, 0)]
+        keys = jnp.concatenate([own_keys(at)] + [early_keys(one, b) for one in early], axis=0)
+        chains([(b, keys, turned_values([at] + early), bias, False)])
+
+        @pl.when(j < 2)
+        def _():
+            arrive(2 + j, 2)
+        return 0
+
+    lax.fori_loop(0, NY, own_work, 0)
+
+    def block_work(b, ways, step):
+        slots = []
+        for way in ways:
+            shift = shift_of(way, step)
+            there = lax.rem(z + shift + NZ, NZ)
+            slots += [slot(b - 1, shift), slot(jnp.where(there < z, b, b - 2), shift)]
+        keys = jnp.concatenate([early_keys(at, b) for at in slots], axis=0)
+        chains([(b, keys, turned_values(slots), None, True)])
 
     def wait_for_x(step):
         for way in range(2):
@@ -365,18 +362,17 @@
 
     def later_step(step, _):
         def catch_up(j, _):
-            @pl.when(j == 1)
+            @pl.when(step < half - 1)
+            def _():
+                arrive(j, step + 2)
+
+            @pl.when(j == 2)
             def _():
                 wait_for_x(step)
-            pair_work(1 - j, (0, 1), step)
-
-            @pl.when(step < half - 1)
-            def _():
-                arrive(2 * j, step + 2)
-                arrive(2 * j + 1, step + 2)
+            block_work(NY - 1 - j, (0, 1), step)
             return 0
 
-        lax.fori_loop(0, 2 - step // (half - 1), catch_up, 0)
+        lax.fori_loop(0, NY - 2 * (step // (half - 1)), catch_up, 0)
         return 0
 
     lax.fori_loop(1, half, later_step, 0)
@@ -434,26 +430,31 @@
     early = (y == 1) | (y == 2)
 
     def finish(j, _):
-        @pl.when(j == 1)
+        @pl.when(j == 2)
         def _():
             wait_for_x(half - 1)
-            pair_work(0, (0, 1), half - 1)
-
-            @pl.when(early)
-            def _():
-                output_through(4)
-
-            @pl.when(jnp.logical_not(early))
-            def _():
-                output_through(5)
+
+        @pl.when(j >= 2)
+        def _():
+            block_work(NY - 1 - j, (0, 1), half - 1)
+
+        @pl.when(j == 2)
+        def _():
             for row in (NY - 1, NY - 2):
                 wait_x(row, last_way(row), half)
-        pair_work(1 - j, (0,), half)
-        for i in (1, 0):
-            send_back(2 * (1 - j) + i)
-        return 0
-
-    lax.fori_loop(0, 2, finish, 0)
+
+        @pl.when((j == 3) & early)
+        def _():
+            output_through(4)
+
+        @pl.when((j == 3) & jnp.logical_not(early))
+        def _():
+            output_through(5)
+        block_work(NY - 1 - j, (0,), half)
+        send_back(NY - 1 - j)
+        return 0
+
+    lax.fori_loop(0, NY, finish, 0)
 
     @pl.when(early)
     def _():

time: 85 us -> 86.7 us (1.020)
  Pallas kernels: 83.9 us -> 85.6 us
    pallas_call x1, Pallas kernels: 83.9 us -> 85.6 us  [per_device(): pl.pallas_call(attention_kernel, out_shape=jax.ShapeDtypeStruct((TOK // 2...]
where the time goes in v11:
time: 86.7 us; the launch traced here: 86.6 us
  Pallas kernels  85.6 us (99%)
  local copies, waits for them, and re-layouts  0.97 us (1%)
    pallas_call x1, Pallas kernels, per_device(): pl.pallas_call(attention_kernel, out_shape=jax.ShapeDtypeStruct((TOK // 2...  85.6 us

profile of v11, /device:TPU:6, one launch (start us, length us, event | category | flops | bytes accessed | tf_op | source)
XLA Modules:
  0.0 86.6 jit_solution(12783588312768627745)
XLA Ops:
  0.0 85.6 %attention.1 = bf16[128,4096]{1,0:T(8,128)(2,1)S(1)} custom-call(bf16[256,2048]{1,0:T(8,128)(2,1)} %q_ref.1, bf16[256,512]{1,0:T(8,128)(2,1)} %k_ref.1, bf16[256,512]{1,0:T(8,128)(2,1)} %v_ref.1, s32[2,128]{1,0:T(2,128)} %bitcast.1), custom_call_target="tpu_custom_call" | custom-call | tf_op jit(solution)/shard_map/attention/pallas_call | solution.py:516
  85.6 1.0 %copy.6 = bf16[128,4096]{1,0:T(8,128)(2,1)} copy(bf16[128,4096]{1,0:T(8,128)(2,1)S(1)} %attention.1) | data formatting | bytes 2097152

commit v12 on v4

--- a/solution.py
+++ b/solution.py
@@ -36,7 +36,8 @@
 def attention_kernel(q_ref, k_ref, v_ref, seg_ref, out_ref, q_buf, v_buf, seg_in, seg_buf, vt_buf, qt_buf,
                      kv, qe, acc, peak, first, o_buf, load_sem,
                      y_send, y_recv, q_send, q_recv, z_send, z_recv, x_send, x_recv,
-                     side_send, side_recv, ready, o_send, o_recv):
+                     side_send, side_recv, ready, o_send, o_recv,
+                     q_box, o_box, r_send, r_recv, f_send):
     me, x, y, z = place()
     core = lax.axis_index("kvh")
     half = NZ // 2
@@ -97,6 +98,20 @@
             copy.start()
             sent.append(copy)
 
+    up, across, down = y_peers
+    up_dev, down_dev = dev(x, up, z), dev(x, down, z)
+
+    def through(part, src, box):
+        return remote(src, box, r_send.at[part - 2], r_recv.at[part - 2], down_dev if part % 2 else up_dev)
+
+    def send(copy):
+        copy.start()
+        sent.append(copy)
+
+    def pass_through(part, box, dst, recv, device):
+        pltpu.make_async_copy(box, box, r_recv.at[part - 2]).wait()
+        send(remote(box, dst, f_send.at[part - 2], recv, device))
+
     def shift_of(way, step):
         return step * (2 * way - 1)
 
@@ -163,9 +178,12 @@
         for g in range(GROUP):
             h = p * GROUP + g
             qt_buf[p, :, g * TOK:(g + 1) * TOK] = q_buf[:, h * DIM:(h + 1) * DIM].T
+    part_rows = DIM // 2
+    send(through(2, qt_buf.at[across, pl.ds(0, part_rows)], q_box.at[0]))
+    send(through(3, qt_buf.at[across, pl.ds(part_rows, part_rows)], q_box.at[1]))
     asked = []
-    for n, p in enumerate(y_peers):
-        copy = remote(qt_buf.at[p], qe.at[y, pl.ds(0, DIM)], q_send.at[n], q_recv.at[n], dev(x, p, z))
+    for n in (0, 2):
+        copy = remote(qt_buf.at[y_peers[n]], qe.at[y, pl.ds(0, DIM)], q_send.at[n], q_recv.at[n], dev(x, y_peers[n], z))
         copy.start()
         asked.append(copy)
     own_q = pltpu.make_async_copy(qt_buf.at[y], qe.at[y, pl.ds(0, DIM)], q_send.at[NY - 1])
@@ -192,7 +210,10 @@
         arrive(i, 1)
         return 0
 
-    lax.fori_loop(0, NY, first_step, 0)
+    lax.fori_loop(0, 2, first_step, 0)
+    pass_through(2, q_box.at[0], qe.at[down, pl.ds(0, part_rows)], q_recv.at[1], up_dev)
+    pass_through(3, q_box.at[1], qe.at[up, pl.ds(part_rows, part_rows)], q_recv.at[1], down_dev)
+    lax.fori_loop(2, NY, first_step, 0)
 
     def wait_x(row, way, step):
         @pl.when(over_x(way, row, step) & (x > 0))
@@ -207,6 +228,8 @@
             side_copy(way).start()
     for copy in asked:
         copy.wait_recv()
+    far_q = qe.at[across, pl.ds(0, DIM)]
+    pltpu.make_async_copy(far_q, far_q, q_recv.at[1]).wait()
     own_q.wait()
 
     key = lax.broadcasted_iota(jnp.int32, (TOK, TOK), 0)
@@ -343,15 +366,37 @@
         mixed = (acc[b, :DIM, :] * (1.0 / acc[b, DIM:DIM + 1, :])).astype(jnp.bfloat16)
         for g in range(GROUP):
             o_buf[b, :, g * DIM:(g + 1) * DIM] = mixed[:, g * TOK:(g + 1) * TOK].T
-        over(b).start()
-
-        @pl.when(b != y)
+
+        @pl.when(b == across)
+        def _():
+            through(4, part(b, core), o_box.at[0]).start()
+            through(5, part(b, 1 - core), o_box.at[1]).start()
+
+        @pl.when(b != across)
+        def _():
+            over(b).start()
+
+        @pl.when((b != across) & (b != y))
         def _():
             along(b).start()
 
         @pl.when(b == y)
         def _():
             stay(b).start()
+
+    def cols_of(source):
+        return out_ref.at[:, pl.ds(pl.multiple_of((core * NY + source) * wide, wide), wide)]
+
+    def output_through(part):
+        pltpu.make_async_copy(o_box.at[part - 4], o_box.at[part - 4], r_recv.at[part - 2]).wait()
+        output_on(part).start()
+
+    def output_on(part):
+        if part == 4:
+            return remote(o_box.at[0], cols_of(down), f_send.at[2], o_recv.at[down, 0], up_dev)
+        return remote(o_box.at[1], cols_of(up), f_send.at[3], o_recv.at[up, 1], (index_of(x, down, z), 1 - core))
+
+    early = (y == 1) | (y == 2)
 
     def finish(j, _):
         @pl.when(j == 1)
@@ -365,6 +410,16 @@
 
     lax.fori_loop(0, 2, finish, 0)
 
+    @pl.when(early)
+    def _():
+        output_through(4)
+        output_through(5)
+
+    @pl.when(jnp.logical_not(early))
+    def _():
+        output_through(5)
+        output_through(4)
+
     for copy in sent + asked:
         copy.wait_send()
 
@@ -392,10 +447,16 @@
         @pl.when(side_goes(way))
         def _():
             side_copy(way).wait_send()
+    through(4, part(across, core), o_box.at[0]).wait_send()
+    through(5, part(across, 1 - core), o_box.at[1]).wait_send()
+    output_on(4).wait_send()
+    output_on(5).wait_send()
     for b in range(NY):
-        over(b).wait_send()
-
-        @pl.when(b != y)
+        @pl.when(b != across)
+        def _():
+            over(b).wait_send()
+
+        @pl.when((b != y) & (b != across))
         def _():
             along(b).wait_send()
         for e in range(2):
@@ -421,7 +482,9 @@
             pltpu.VMEM((NY, 8, 128), f32), pltpu.VMEM((NY, TOK, GROUP * DIM), bf16),
             dma((3,)), dma((NY - 1, 3)), dma((NY,)), dma((NY,)), dma((NY - 1,)),
             dma((2, NY, half)), dma((2, NY, half)), dma((BACK, 2, half + 1)), dma((BACK, 2, half + 1)),
-            dma((2,)), dma((2,)), pltpu.SemaphoreType.REGULAR, dma((NY, 2)), dma((NY, 2))],
+            dma((2,)), dma((2,)), pltpu.SemaphoreType.REGULAR, dma((NY, 2)), dma((NY, 2)),
+            pltpu.VMEM((2, DIM // 2, LANES), bf16), pltpu.VMEM((2, TOK // 2, GROUP * DIM), bf16),
+            dma((4,)), dma((4,)), dma((4,))],
         compiler_params=pltpu.CompilerParams(collective_id=0, has_side_effects=True,
                                              vmem_limit_bytes=40 * 1024 * 1024),
         name="attention",

time: 84.7 us -> 85.5 us (level)
  Pallas kernels: 83.5 us -> 84.5 us
    pallas_call x1, Pallas kernels: 83.5 us -> 84.5 us  [per_device(): pl.pallas_call(attention_kernel, out_shape=jax.ShapeDtypeStruct((TOK // 2...]
where the time goes in v12:
time: 85.5 us; the launch traced here: 85.4 us
  Pallas kernels  84.5 us (99%)
  local copies, waits for them, and re-layouts  0.97 us (1%)
    pallas_call x1, Pallas kernels, per_device(): pl.pallas_call(attention_kernel, out_shape=jax.ShapeDtypeStruct((TOK // 2...  84.5 us

profile of v12, /device:TPU:6, one launch (start us, length us, event | category | flops | bytes accessed | tf_op | source)
XLA Modules:
  0.0 85.4 jit_solution(15252459758595032233)
XLA Ops:
  0.0 84.5 %attention.1 = bf16[128,4096]{1,0:T(8,128)(2,1)S(1)} custom-call(bf16[256,2048]{1,0:T(8,128)(2,1)} %q_ref.1, bf16[256,512]{1,0:T(8,128)(2,1)} %k_ref.1, bf16[256,512]{1,0:T(8,128)(2,1)} %v_ref.1, s32[2,128]{1,0:T(2,128)} %bitcast.1), custom_call_target="tpu_custom_call" | custom-call | tf_op jit(solution)/shard_map/attention/pallas_call | solution.py:472
  84.5 1.0 %copy.6 = bf16[128,4096]{1,0:T(8,128)(2,1)} copy(bf16[128,4096]{1,0:T(8,128)(2,1)S(1)} %attention.1) | data formatting | bytes 2097152

commit v13 on v4

--- a/solution.py
+++ b/solution.py
@@ -181,7 +181,7 @@
         lax.fori_loop(0, BACK * NZ, blank, 0)
 
     def arrive(i, step):
-        row = row_of(i)
+        row = NY - 1 - i
         for way in range(2):
             @pl.when((step < half) | (way == last_way(row)))
             def _():

time: 84.7 us -> 84.7 us (level)
  no operation moved by 1% of the time
where the time goes in v13:
time: 84.7 us; the launch traced here: 84.4 us
  Pallas kernels  83.5 us (99%)
  local copies, waits for them, and re-layouts  0.97 us (1%)
    pallas_call x1, Pallas kernels, per_device(): pl.pallas_call(attention_kernel, out_shape=jax.ShapeDtypeStruct((TOK // 2...  83.5 us

profile of v13, /device:TPU:6, one launch (start us, length us, event | category | flops | bytes accessed | tf_op | source)
XLA Modules:
  0.0 84.4 jit_solution(8750653637051892176)
XLA Ops:
  0.0 83.5 %attention.1 = bf16[128,4096]{1,0:T(8,128)(2,1)S(1)} custom-call(bf16[256,2048]{1,0:T(8,128)(2,1)} %q_ref.1, bf16[256,512]{1,0:T(8,128)(2,1)} %k_ref.1, bf16[256,512]{1,0:T(8,128)(2,1)} %v_ref.1, s32[2,128]{1,0:T(2,128)} %bitcast.1), custom_call_target="tpu_custom_call" | custom-call | tf_op jit(solution)/shard_map/attention/pallas_call | solution.py:411
  83.5 1.0 %copy.6 = bf16[128,4096]{1,0:T(8,128)(2,1)} copy(bf16[128,4096]{1,0:T(8,128)(2,1)S(1)} %attention.1) | data formatting | bytes 2097152

commit v14 on v13

--- a/solution.py
+++ b/solution.py
@@ -33,7 +33,7 @@
                                         device_id=device, device_id_type=pl.DeviceIdType.MESH)
 
 
-def attention_kernel(q_ref, k_ref, v_ref, seg_ref, out_ref, q_buf, v_buf, seg_in, seg_buf, vt_buf, qt_buf,
+def attention_kernel(q_ref, k_ref, v_ref, seg_ref, out_ref, q_buf, v_buf, seg_in, seg_buf, vt_buf,
                      kv, qe, acc, peak, first, o_buf, load_sem,
                      y_send, y_recv, q_send, q_recv, z_send, z_recv, x_send, x_recv,
                      side_send, side_recv, ready, o_send, o_recv):
@@ -57,11 +57,9 @@
     def _():
         pl.semaphore_signal(barrier, inc=1, device_id=dev(x_next, y, z), device_id_type=pl.DeviceIdType.MESH)
     load_v = pltpu.make_async_copy(v_ref, v_buf, load_sem.at[0])
-    load_q = pltpu.make_async_copy(q_ref, q_buf, load_sem.at[1])
     load_ids = pltpu.make_async_copy(seg_ref, seg_in, load_sem.at[2])
     load_ids.start()
     load_v.start()
-    load_q.start()
 
     load_ids.wait()
     ids = seg_in[...].astype(jnp.float32)
@@ -73,6 +71,9 @@
 
     def head_cols(p):
         return pl.ds(pl.multiple_of(p * DIM, DIM), DIM)
+
+    def query_cols(p):
+        return pl.ds(pl.multiple_of(p * GROUP * DIM, GROUP * DIM), GROUP * DIM)
 
     mine = (BACK + y) * NZ + z
     pltpu.make_async_copy(k_ref.at[:, head_cols(y)], kv.at[mine, pl.ds(0, TOK)], y_recv.at[y]).start()
@@ -158,17 +159,12 @@
         pl.semaphore_wait(ready, 1)
     forward(0, NY - 1, 0)
     forward(0, NY - 2, 0)
-    load_q.wait()
-    for p in range(NY):
-        for g in range(GROUP):
-            h = p * GROUP + g
-            qt_buf[p, :, g * TOK:(g + 1) * TOK] = q_buf[:, h * DIM:(h + 1) * DIM].T
     asked = []
     for n, p in enumerate(y_peers):
-        copy = remote(qt_buf.at[p], qe.at[y, pl.ds(0, DIM)], q_send.at[n], q_recv.at[n], dev(x, p, z))
+        copy = remote(q_ref.at[:, query_cols(p)], q_buf.at[y], q_send.at[n], q_recv.at[n], dev(x, p, z))
         copy.start()
         asked.append(copy)
-    own_q = pltpu.make_async_copy(qt_buf.at[y], qe.at[y, pl.ds(0, DIM)], q_send.at[NY - 1])
+    own_q = pltpu.make_async_copy(q_ref.at[:, query_cols(y)], q_buf.at[y], q_send.at[NY - 1])
     own_q.start()
 
     @pl.when(x == 0)
@@ -238,7 +234,7 @@
         for i in range(count + 2):
             if i < count:
                 b, cols, keys, _, _, _ = todo[i]
-                scores[i] = jnp.dot(keys, qe[b, :, cols], preferred_element_type=jnp.float32)
+                scores[i] = lax.dot_general(keys, qe[b, cols, :], (((1,), (1,)), ((), ())), preferred_element_type=jnp.float32)
             if 0 <= i - 1 < count:
                 b, cols, _, _, bias, going = todo[i - 1]
                 s = scores[i - 1]
@@ -271,10 +267,13 @@
             rows = jnp.broadcast_to(row, (TOK, TOK))
             begin = row[:, 0:1]
             first[b] = jnp.broadcast_to(begin, (8, 128))
-            rest = jnp.concatenate([jnp.where(row == begin, 0.0, NEG)] * GROUP, axis=1)
-            which = lax.broadcasted_iota(jnp.int32, (DIM, LANES), 0)
-            qe[b, DIM:, :] = jnp.where(which == 0, 1.0, jnp.where(which == 1, rest, 0.0)).astype(jnp.bfloat16)
-            bias = jnp.where((rows == rows.T) & (key <= token), 0.0, NEG)
+            columns = rows.T
+            rest = jnp.where(columns[:, :DIM] == begin, 0.0, NEG)
+            extra = jnp.where(lane == 0, 1.0, jnp.where(lane == 1, rest, 0.0)).astype(jnp.bfloat16)
+            for g in range(GROUP):
+                qe[b, g * TOK:(g + 1) * TOK, :DIM] = q_buf[b, :, g * DIM:(g + 1) * DIM]
+                qe[b, g * TOK:(g + 1) * TOK, DIM:] = extra
+            bias = jnp.where((rows == columns) & (key <= token), 0.0, NEG)
             early = [slot(b - 1, 0), slot(b - 2, 0)]
             keys = jnp.concatenate([own_keys(at)] + [early_keys(one, b) for one in early], axis=0)
             jobs.append((b, keys, turned_values([at] + early), bias, False))
@@ -414,10 +413,10 @@
         in_specs=[hbm_spec] * 4,
         out_specs=any_spec,
         scratch_shapes=[
-            pltpu.VMEM(queries.shape, bf16), pltpu.VMEM(values.shape, bf16), pltpu.VMEM((2, 128), jnp.int32), pltpu.VMEM((16, 128), bf16),
-            pltpu.VMEM((NY, 2 * DIM, TOK // 2), bf16), pltpu.VMEM((NY, DIM, LANES), bf16),
+            pltpu.VMEM((NY, TOK, GROUP * DIM), bf16), pltpu.VMEM(values.shape, bf16), pltpu.VMEM((2, 128), jnp.int32), pltpu.VMEM((16, 128), bf16),
+            pltpu.VMEM((NY, 2 * DIM, TOK // 2), bf16),
             pltpu.VMEM((SLOTS, SLOT_ROWS, DIM), bf16),
-            pltpu.VMEM((NY, 2 * DIM, LANES), bf16), pltpu.VMEM((NY, DIM + 16, LANES), f32), pltpu.VMEM((NY, 8, LANES), f32),
+            pltpu.VMEM((NY, LANES, 2 * DIM), bf16), pltpu.VMEM((NY, DIM + 16, LANES), f32), pltpu.VMEM((NY, 8, LANES), f32),
             pltpu.VMEM((NY, 8, 128), f32), pltpu.VMEM((NY, TOK, GROUP * DIM), bf16),
             dma((3,)), dma((NY - 1, 3)), dma((NY,)), dma((NY,)), dma((NY - 1,)),
             dma((2, NY, half)), dma((2, NY, half)), dma((BACK, 2, half + 1)), dma((BACK, 2, half + 1)),

time: 84.7 us -> 85.1 us (level)
  no operation moved by 1% of the time
where the time goes in v14:
time: 85.1 us; the launch traced here: 84.8 us
  Pallas kernels  83.9 us (99%)
  local copies, waits for them, and re-layouts  0.97 us (1%)
    pallas_call x1, Pallas kernels, per_device(): pl.pallas_call(attention_kernel, out_shape=jax.ShapeDtypeStruct((TOK // 2...  83.9 us

profile of v14, /device:TPU:6, one launch (start us, length us, event | category | flops | bytes accessed | tf_op | source)
XLA Modules:
  0.0 84.8 jit_solution(2436600040182373962)
XLA Ops:
  0.0 83.9 %attention.1 = bf16[128,4096]{1,0:T(8,128)(2,1)S(1)} custom-call(bf16[256,2048]{1,0:T(8,128)(2,1)} %q_ref.1, bf16[256,512]{1,0:T(8,128)(2,1)} %k_ref.1, bf16[256,512]{1,0:T(8,128)(2,1)} %v_ref.1, s32[2,128]{1,0:T(2,128)} %bitcast.1), custom_call_target="tpu_custom_call" | custom-call | tf_op jit(solution)/shard_map/attention/pallas_call | solution.py:410
  83.9 1.0 %copy.6 = bf16[128,4096]{1,0:T(8,128)(2,1)} copy(bf16[128,4096]{1,0:T(8,128)(2,1)S(1)} %attention.1) | data formatting | bytes 2097152

commit v15 on v13

--- a/solution.py
+++ b/solution.py
@@ -14,6 +14,8 @@
 SLOTS = ROWS * NZ
 SLOT_ROWS = 2 * TOK + 16
 LANES = GROUP * TOK
+WIDE = LANES
+PIECES = 2
 NEG = -1e30
 FAR_ID = 512.0
 SCALE = 1.4426950408889634 * DIM ** -0.5
@@ -231,35 +233,56 @@
         return jnp.concatenate([vt, jnp.ones((16, vt.shape[1]), jnp.bfloat16)], axis=0)
 
     def chains(jobs):
-        todo = [(b, slice(g * TOK, (g + 1) * TOK), keys, vt, bias, going)
-                for b, keys, vt, bias, going in jobs for g in range(GROUP)]
+        todo = [(b, slice(g * WIDE, (g + 1) * WIDE), keys, vt, bias, going)
+                for b, keys, vt, bias, going in jobs for g in range(LANES // WIDE)]
         count = len(todo)
-        scores, weights, done = [None] * count, [None] * count, []
-        for i in range(count + 2):
-            if i < count:
-                b, cols, keys, _, _, _ = todo[i]
-                scores[i] = jnp.dot(keys, qe[b, :, cols], preferred_element_type=jnp.float32)
-            if 0 <= i - 1 < count:
-                b, cols, _, _, bias, going = todo[i - 1]
-                s = scores[i - 1]
-                if bias is not None:
-                    s = jnp.concatenate([s[:TOK] + bias, s[TOK:]], axis=0)
-                new = jnp.max(s, axis=0, keepdims=True)
-                fade = None
-                if going:
-                    old = peak[b, 0:1, cols]
-                    new = jnp.maximum(old, new)
-                    fade = jnp.exp2((old - new) * SCALE)
-                weights[i - 1] = (jnp.exp2((s - new) * SCALE).astype(jnp.bfloat16), new, fade)
-                scores[i - 1] = None
-            if i >= 2:
-                b, cols, _, vt, _, going = todo[i - 2]
-                w, new, fade = weights[i - 2]
-                done.append((b, cols, new, fade, jnp.dot(vt, w, preferred_element_type=jnp.float32)))
-                weights[i - 2] = None
-        for b, cols, new, fade, o in done:
+
+        def scores_of(i, n):
+            b, cols, keys, _, bias, _ = todo[i]
+            size = keys.shape[0] // PIECES
+            s = jnp.dot(keys[n * size:(n + 1) * size], qe[b, :, cols], preferred_element_type=jnp.float32)
+            if bias is not None and n == 0:
+                s = jnp.concatenate([s[:TOK] + bias, s[TOK:]], axis=0)
+            return s, jnp.max(s, axis=0, keepdims=True)
+
+        def weigh(i, n, s, shift):
+            return jnp.exp2(s * SCALE - shift).astype(jnp.bfloat16)
+
+        def values_of(i, n, w, o):
+            vt = todo[i][3]
+            size = vt.shape[1] // PIECES
+            more = jnp.dot(vt[:, n * size:(n + 1) * size], w, preferred_element_type=jnp.float32)
+            return more if o is None else o + more
+
+        ahead = [scores_of(0, n) for n in range(PIECES)]
+        late = None
+        for i, (b, cols, keys, vt, bias, going) in enumerate(todo):
+            held, ahead = ahead, []
+            new = held[0][1]
+            for _, top in held[1:]:
+                new = jnp.maximum(new, top)
+            fade = None
+            if going:
+                old = peak[b, 0:1, cols]
+                new = jnp.maximum(old, new)
+                fade = jnp.exp2((old - new) * SCALE)
             peak[b, 0:1, cols] = new
-            acc[b, :, cols] = o if fade is None else acc[b, :, cols] * fade + o
+            shift = new * SCALE
+            o = None
+            for n in range(PIECES):
+                if i + 1 < count:
+                    ahead.append(scores_of(i + 1, n))
+                w = weigh(i, n, held[n][0], shift)
+                if late is not None:
+                    late()
+                    late = None
+                if n + 1 < PIECES:
+                    o = values_of(i, n, w, o)
+
+            def late(i=i, w=w, o=o, b=b, cols=cols, fade=fade):
+                total = values_of(i, PIECES - 1, w, o)
+                acc[b, :, cols] = total if fade is None else acc[b, :, cols] * fade + total
+        late()
 
     def own_work(j, _):
         jobs = []
@@ -274,7 +297,7 @@
             rest = jnp.concatenate([jnp.where(row == begin, 0.0, NEG)] * GROUP, axis=1)
             which = lax.broadcasted_iota(jnp.int32, (DIM, LANES), 0)
             qe[b, DIM:, :] = jnp.where(which == 0, 1.0, jnp.where(which == 1, rest, 0.0)).astype(jnp.bfloat16)
-            bias = jnp.where((rows == rows.T) & (key <= token), 0.0, NEG)
+            bias = jnp.concatenate([jnp.where((rows == rows.T) & (key <= token), 0.0, NEG)] * (WIDE // TOK), axis=1)
             early = [slot(b - 1, 0), slot(b - 2, 0)]
             keys = jnp.concatenate([own_keys(at)] + [early_keys(one, b) for one in early], axis=0)
             jobs.append((b, keys, turned_values([at] + early), bias, False))
@@ -283,13 +306,15 @@
 
     lax.fori_loop(0, NY // 2, own_work, 0)
 
-    def pair_work(pair, way, step):
-        shift = shift_of(way, step)
-        there = lax.rem(z + shift + NZ, NZ)
+    def pair_work(pair, ways, step):
         jobs = []
         for i in (1, 0):
             b = 2 * pair + i
-            slots = [slot(b - 1, shift), slot(jnp.where(there < z, b, b - 2), shift)]
+            slots = []
+            for way in ways:
+                shift = shift_of(way, step)
+                there = lax.rem(z + shift + NZ, NZ)
+                slots += [slot(b - 1, shift), slot(jnp.where(there < z, b, b - 2), shift)]
             keys = jnp.concatenate([early_keys(at, b) for at in slots], axis=0)
             jobs.append((b, keys, turned_values(slots), None, True))
         chains(jobs)
@@ -298,9 +323,10 @@
         def catch_up(j, _):
             @pl.when(step < half - 1)
             def _():
-                arrive(j, step + 1)
-
-            @pl.when(j == 2)
+                arrive(2 * j, step + 1)
+                arrive(2 * j + 1, step + 1)
+
+            @pl.when(j == 1)
             def _():
                 for way in range(2):
                     for row in (NY - 1, NY - 2):
@@ -309,10 +335,10 @@
                     @pl.when((step == 1) & side_comes(way))
                     def _():
                         side_copy(way).wait_recv()
-            pair_work(1 - j // 2, j % 2, step)
+            pair_work(1 - j, (0, 1), step)
             return 0
 
-        lax.fori_loop(0, 4, catch_up, 0)
+        lax.fori_loop(0, 2, catch_up, 0)
         return 0
 
     lax.fori_loop(1, half, later_step, 0)
@@ -358,7 +384,7 @@
         def _():
             for row in (NY - 1, NY - 2):
                 wait_x(row, last_way(row), half)
-        pair_work(1 - j, 0, half)
+        pair_work(1 - j, (0,), half)
         for i in (1, 0):
             send_back(2 * (1 - j) + i)
         return 0

time: 84.7 us -> 84 us (level)
  no operation moved by 1% of the time
where the time goes in v15:
time: 84 us; the launch traced here: 83.7 us
  Pallas kernels  82.7 us (98%)
  local copies, waits for them, and re-layouts  0.97 us (1%)
    pallas_call x1, Pallas kernels, per_device(): pl.pallas_call(attention_kernel, out_shape=jax.ShapeDtypeStruct((TOK // 2...  82.7 us

profile of v15, /device:TPU:6, one launch (start us, length us, event | category | flops | bytes accessed | tf_op | source)
XLA Modules:
  0.0 83.7 jit_solution(2571353305916207569)
XLA Ops:
  0.0 82.7 %attention.1 = bf16[128,4096]{1,0:T(8,128)(2,1)S(1)} custom-call(bf16[256,2048]{1,0:T(8,128)(2,1)} %q_ref.1, bf16[256,512]{1,0:T(8,128)(2,1)} %k_ref.1, bf16[256,512]{1,0:T(8,128)(2,1)} %v_ref.1, s32[2,128]{1,0:T(2,128)} %bitcast.1), custom_call_target="tpu_custom_call" | custom-call | tf_op jit(solution)/shard_map/attention/pallas_call | solution.py:437
  82.7 1.0 %copy.6 = bf16[128,4096]{1,0:T(8,128)(2,1)} copy(bf16[128,4096]{1,0:T(8,128)(2,1)S(1)} %attention.1) | data formatting | bytes 2097152

commit v16 on v15

--- a/solution.py
+++ b/solution.py
@@ -38,7 +38,8 @@
 def attention_kernel(q_ref, k_ref, v_ref, seg_ref, out_ref, q_buf, v_buf, seg_in, seg_buf, vt_buf, qt_buf,
                      kv, qe, acc, peak, first, o_buf, load_sem,
                      y_send, y_recv, q_send, q_recv, z_send, z_recv, x_send, x_recv,
-                     side_send, side_recv, ready, o_send, o_recv):
+                     side_send, side_recv, ready, o_send, o_recv,
+                     o_box, r_send, r_recv, f_send):
     me, x, y, z = place()
     core = lax.axis_index("kvh")
     half = NZ // 2
@@ -98,6 +99,12 @@
             copy = remote(src, kv.at[mine, pl.ds(lo, rows)], y_send.at[n, i], y_recv.at[y], dev(x, p, z))
             copy.start()
             sent.append(copy)
+
+    up, across, down = y_peers
+    up_dev, down_dev = dev(x, up, z), dev(x, down, z)
+
+    def through(part, src, box):
+        return remote(src, box, r_send.at[part - 4], r_recv.at[part - 4], down_dev if part % 2 else up_dev)
 
     def shift_of(way, step):
         return step * (2 * way - 1)
@@ -369,15 +376,37 @@
         mixed = (acc[b, :DIM, :] * (1.0 / acc[b, DIM:DIM + 1, :])).astype(jnp.bfloat16)
         for g in range(GROUP):
             o_buf[b, :, g * DIM:(g + 1) * DIM] = mixed[:, g * TOK:(g + 1) * TOK].T
-        over(b).start()
-
-        @pl.when(b != y)
+
+        @pl.when(b == across)
+        def _():
+            through(4, part(b, core), o_box.at[0]).start()
+            through(5, part(b, 1 - core), o_box.at[1]).start()
+
+        @pl.when(b != across)
+        def _():
+            over(b).start()
+
+        @pl.when((b != across) & (b != y))
         def _():
             along(b).start()
 
         @pl.when(b == y)
         def _():
             stay(b).start()
+
+    def cols_of(source):
+        return out_ref.at[:, pl.ds(pl.multiple_of((core * NY + source) * wide, wide), wide)]
+
+    def output_through(part):
+        pltpu.make_async_copy(o_box.at[part - 4], o_box.at[part - 4], r_recv.at[part - 4]).wait()
+        output_on(part).start()
+
+    def output_on(part):
+        if part == 4:
+            return remote(o_box.at[0], cols_of(down), f_send.at[0], o_recv.at[down, 0], up_dev)
+        return remote(o_box.at[1], cols_of(up), f_send.at[1], o_recv.at[up, 1], (index_of(x, down, z), 1 - core))
+
+    early = (y == 1) | (y == 2)
 
     def finish(j, _):
         @pl.when(j == 1)
@@ -391,6 +420,16 @@
 
     lax.fori_loop(0, 2, finish, 0)
 
+    @pl.when(early)
+    def _():
+        output_through(4)
+        output_through(5)
+
+    @pl.when(jnp.logical_not(early))
+    def _():
+        output_through(5)
+        output_through(4)
+
     for copy in sent + asked:
         copy.wait_send()
 
@@ -418,10 +457,16 @@
         @pl.when(side_goes(way))
         def _():
             side_copy(way).wait_send()
+    through(4, part(across, core), o_box.at[0]).wait_send()
+    through(5, part(across, 1 - core), o_box.at[1]).wait_send()
+    output_on(4).wait_send()
+    output_on(5).wait_send()
     for b in range(NY):
-        over(b).wait_send()
-
-        @pl.when(b != y)
+        @pl.when(b != across)
+        def _():
+            over(b).wait_send()
+
+        @pl.when((b != y) & (b != across))
         def _():
             along(b).wait_send()
         for e in range(2):
@@ -447,7 +492,8 @@
             pltpu.VMEM((NY, 8, 128), f32), pltpu.VMEM((NY, TOK, GROUP * DIM), bf16),
             dma((3,)), dma((NY - 1, 3)), dma((NY,)), dma((NY,)), dma((NY - 1,)),
             dma((2, NY, half)), dma((2, NY, half)), dma((BACK, 2, half + 1)), dma((BACK, 2, half + 1)),
-            dma((2,)), dma((2,)), pltpu.SemaphoreType.REGULAR, dma((NY, 2)), dma((NY, 2))],
+            dma((2,)), dma((2,)), pltpu.SemaphoreType.REGULAR, dma((NY, 2)), dma((NY, 2)),
+            pltpu.VMEM((2, TOK // 2, GROUP * DIM), bf16), dma((2,)), dma((2,)), dma((2,))],
         compiler_params=pltpu.CompilerParams(collective_id=0, has_side_effects=True,
                                              vmem_limit_bytes=40 * 1024 * 1024),
         name="attention",

time: 84 us -> 84.8 us (level)
  Pallas kernels: 82.7 us -> 83.7 us
    pallas_call x1, Pallas kernels: 82.7 us -> 83.7 us  [per_device(): pl.pallas_call(attention_kernel, out_shape=jax.ShapeDtypeStruct((TOK // 2...]
where the time goes in v16:
time: 84.8 us; the launch traced here: 84.6 us
  Pallas kernels  83.7 us (99%)
  local copies, waits for them, and re-layouts  0.97 us (1%)
    pallas_call x1, Pallas kernels, per_device(): pl.pallas_call(attention_kernel, out_shape=jax.ShapeDtypeStruct((TOK // 2...  83.7 us

profile of v16, /device:TPU:6, one launch (start us, length us, event | category | flops | bytes accessed | tf_op | source)
XLA Modules:
  0.0 84.6 jit_solution(8209250890436824744)
XLA Ops:
  0.0 83.7 %attention.1 = bf16[128,4096]{1,0:T(8,128)(2,1)S(1)} custom-call(bf16[256,2048]{1,0:T(8,128)(2,1)} %q_ref.1, bf16[256,512]{1,0:T(8,128)(2,1)} %k_ref.1, bf16[256,512]{1,0:T(8,128)(2,1)} %v_ref.1, s32[2,128]{1,0:T(2,128)} %bitcast.1), custom_call_target="tpu_custom_call" | custom-call | tf_op jit(solution)/shard_map/attention/pallas_call | solution.py:482
  83.7 1.0 %copy.6 = bf16[128,4096]{1,0:T(8,128)(2,1)} copy(bf16[128,4096]{1,0:T(8,128)(2,1)S(1)} %attention.1) | data formatting | bytes 2097152
